TPU v7x, 512 devices: a whole 4x8x8 slice. The times are simulated.
512 devices in a mesh: dp: 16 (over y, core), rule: 32 (over x, z).
Axes of the slice: x: 4, y: 8, z: 8, core: 2. Of those that a mesh axis runs over, the one named last changes fastest.
Arguments:
- hidden_states: bfloat16 [4096, 8192], P(('dp', 'rule')), may hold values from -6 to 6
- attn_input: bfloat16 [4096, 8192], P(('dp', 'rule')), may hold values from -6 to 6
- rule_ids: int32 [4096, 2], replicated, may hold values from 0 to 127, as said below
- slot_ids: int32 [4096, 2], replicated, may hold values from -1 to 127, as said below
- cotangent: bfloat16 [4096, 2], replicated, may hold values from -6 to 6
- adapter_in: bfloat16 [128, 8192, 512], P('dp', 'rule'), may hold values from -0.0625 to 0.0625
- adapter_bias: float32 [128, 512], P('dp'), may hold values from -3 to 3
- adapter_out: float32 [128, 512], P('dp'), may hold values from -0.25 to 0.25
Outputs:
- rewards: bfloat16 [4096, 2], P('dp')
- adapter_in_grad: bfloat16 [128, 8192, 512], P('dp', 'rule')
- adapter_bias_grad: float32 [128, 512], P('dp')
- adapter_out_grad: float32 [128, 512], P('dp')
- o_proj_grad: bfloat16 [8192, 8192], P('rule', 'dp')
Inputs may be any that keep to these rules, and one draw needn't show every extreme that they name: `rule_ids`: the owner of rule r is r // 8. Among the 16 pairs of one block of 8 consecutive tokens at most 2 name rules of any one owner, and in every block some owner gets exactly 2. The two rules of a token differ. slot_ids[t, k] counts the earlier pairs, in the order of t then k, that name the same rule; it is -1 where that count reaches 128. Some rule fills all 128 rows.
All inputs are finite; a program needn't handle non-finite values.
Results may differ from a plain program's by a relative error of at most 0.03.
Values may be sent and summed in bfloat16 or wider, within the bound.
No kernel may reach another device: no remote copies, remote signals or barrier semaphores. Data moves between devices by JAX's collectives and lax.ppermute only.
A program may use at most 64 MiB of HBM per device.

v0:
```python
import jax
import jax.numpy as jnp
from jax import lax
from jax.sharding import PartitionSpec as P


def local(
    hidden_states, attn_input, rule_ids, slot_ids, cotangent, adapter_in, adapter_bias, adapter_out
):
    dp_size = lax.axis_size("dp")
    rule_size = lax.axis_size("rule")
    dp_index = lax.axis_index("dp")
    rule_index = lax.axis_index("rule")
    rows_dev = hidden_states.shape[0]
    adapters, feature_cols, hidden_units = adapter_in.shape
    send_cap = max(2, 4 * rows_dev // dp_size)
    capacity = 4 * rows_dev * rule_size // adapters
    block_count = dp_size * rule_size
    pair_count = 2 * rows_dev
    slot_count = dp_size * send_cap
    recv_count = slot_count * rule_size
    buffer_rows = adapters * capacity
    rule_all = rule_ids.reshape(block_count, pair_count)
    slot_all = slot_ids.reshape(block_count, pair_count)
    cot_all = cotangent.reshape(block_count, pair_count).astype(jnp.float32)
    owner_all = rule_all // adapters
    earlier = jnp.arange(pair_count)[None, :] < jnp.arange(pair_count)[:, None]
    same_owner = owner_all[:, :, None] == owner_all[:, None, :]
    rank_all = jnp.sum((same_owner & earlier[None]).astype(jnp.int32), axis=2)
    my_block = dp_index * rule_size + rule_index
    my_owner = lax.dynamic_index_in_dim(owner_all, my_block, 0, keepdims=False)
    my_rank = lax.dynamic_index_in_dim(rank_all, my_block, 0, keepdims=False)
    target = my_owner * send_cap + my_rank
    select_pairs = (jnp.arange(slot_count)[:, None] == target[None, :]).astype(jnp.int32)
    select_tokens = jnp.sum(select_pairs.reshape(slot_count, rows_dev, 2), axis=2).astype(
        jnp.bfloat16
    )
    outgoing = jnp.dot(select_tokens, hidden_states, preferred_element_type=jnp.float32).astype(
        jnp.bfloat16
    )
    outgoing = outgoing.reshape(dp_size, send_cap, rule_size, feature_cols)
    incoming = lax.all_to_all(
        lax.all_to_all(outgoing, "dp", split_axis=0, concat_axis=0, tiled=True),
        "rule",
        split_axis=2,
        concat_axis=2,
        tiled=True,
    )
    flat_in = jnp.concatenate(
        [incoming.reshape(recv_count, feature_cols), jnp.zeros((1, feature_cols), jnp.bfloat16)],
        axis=0,
    )
    block_dp = (jnp.arange(block_count) // rule_size)[:, None]
    block_rule = (jnp.arange(block_count) % rule_size)[:, None]
    recv_index = (block_dp * send_cap + rank_all) * rule_size + block_rule
    owned = (owner_all == dp_index) & (slot_all >= 0)
    buffer_pos = rule_all % adapters * capacity + slot_all
    pos_target = jnp.where(owned, buffer_pos, buffer_rows).reshape(-1)
    recv_target = jnp.where(owned, recv_index, recv_count).reshape(-1)
    to_recv = (
        jnp.full((buffer_rows + 1,), recv_count, jnp.int32)
        .at[pos_target]
        .set(recv_index.reshape(-1))[:buffer_rows]
    )
    to_buffer = (
        jnp.full((recv_count + 1,), buffer_rows, jnp.int32)
        .at[recv_target]
        .set(buffer_pos.reshape(-1))[:recv_count]
    )
    cot_buffer = (
        jnp.zeros((buffer_rows + 1,), jnp.float32)
        .at[pos_target]
        .set(cot_all.reshape(-1))[:buffer_rows]
    )
    cot_rows = cot_buffer.reshape(adapters, capacity)
    rows_buf = jnp.take(flat_in, to_recv, axis=0).reshape(adapters, capacity, feature_cols)
    partial_pre = jnp.einsum(
        "acd,adr->acr", rows_buf, adapter_in, preferred_element_type=jnp.float32
    )
    preact = (
        lax.psum(partial_pre.astype(jnp.bfloat16), "rule").astype(jnp.float32)
        + adapter_bias[:, None, :]
    )
    sigmoid_z = jax.nn.sigmoid(preact)
    activated = preact * sigmoid_z
    reward_rows = jnp.sum(activated * adapter_out[:, None, :], axis=2)
    grad_pre = (
        cot_rows[:, :, None]
        * adapter_out[:, None, :]
        * sigmoid_z
        * (1.0 + preact * (1.0 - sigmoid_z))
    )
    grad_half = grad_pre.astype(jnp.bfloat16)
    bias_grad = jnp.sum(grad_pre, axis=1)
    out_grad = jnp.sum(cot_rows[:, :, None] * activated, axis=1)
    reward_flat = jnp.concatenate([reward_rows.reshape(-1), jnp.zeros((1,), jnp.float32)]).astype(
        jnp.bfloat16
    )
    in_grad = jnp.einsum(
        "acd,acr->adr", rows_buf, grad_half, preferred_element_type=jnp.float32
    ).astype(jnp.bfloat16)
    input_grad = jnp.einsum(
        "acr,adr->acd", grad_half, adapter_in, preferred_element_type=jnp.float32
    ).astype(jnp.bfloat16)
    grad_flat = jnp.concatenate(
        [input_grad.reshape(buffer_rows, feature_cols), jnp.zeros((1, feature_cols), jnp.bfloat16)],
        axis=0,
    )
    back_rows = jnp.take(grad_flat, to_buffer, axis=0).reshape(
        dp_size, send_cap, rule_size, feature_cols
    )
    back_reward = jnp.take(reward_flat, to_buffer, axis=0).reshape(dp_size, send_cap, rule_size)
    returned, reward_back = (
        lax.all_to_all(back_rows, "dp", split_axis=0, concat_axis=0, tiled=True),
        lax.all_to_all(back_reward, "dp", split_axis=0, concat_axis=0, tiled=True),
    )
    owner_group = lax.dynamic_slice_in_dim(owner_all, dp_index * rule_size, rule_size, 0)
    rank_group = lax.dynamic_slice_in_dim(rank_all, dp_index * rule_size, rule_size, 0)
    pair_index = (
        (owner_group * send_cap + rank_group) * rule_size + jnp.arange(rule_size)[:, None]
    ).reshape(-1)
    pair_grads = jnp.take(returned.reshape(recv_count, feature_cols), pair_index, axis=0)
    pair_grads = pair_grads.astype(jnp.float32).reshape(rule_size * rows_dev, 2, feature_cols)
    state_grad = jnp.sum(pair_grads, axis=1).astype(jnp.bfloat16)
    rewards = jnp.take(reward_back.reshape(recv_count), pair_index, axis=0).reshape(
        rule_size * rows_dev, 2
    )
    group_term = lax.dot_general(
        state_grad,
        lax.all_gather(attn_input, "rule", axis=0, tiled=True),
        (((0,), (0,)), ((), ())),
        preferred_element_type=jnp.float32,
    )
    o_proj_grad = lax.psum_scatter(
        group_term.astype(jnp.bfloat16), "dp", scatter_dimension=1, tiled=True
    )
    return (rewards, in_grad, bias_grad, out_grad, o_proj_grad)


def solution(mesh):
    placed = (
        P(("dp", "rule"), None),
        P(("dp", "rule"), None),
        P(),
        P(),
        P(),
        P("dp", "rule", None),
        P("dp", None),
        P("dp", None),
    )
    return jax.shard_map(
        local,
        mesh=mesh,
        in_specs=placed,
        out_specs=(
            P("dp", None),
            P("dp", "rule", None),
            P("dp", None),
            P("dp", None),
            P("rule", "dp"),
        ),
        check_vma=False,
    )
```

profile of v0, /device:TPU:1, one launch (start us, length us, event | category | flops | bytes accessed | tf_op | source)
XLA Modules:
  0.0 412.3 jit_solution(5841563843183169320)
XLA Ops:
  7.2 2.9 copy.44
  14.8 10.4 %all-to-all-start = ((bf16[16,2,32,256]{3,1,2,0:T(2,128)(2,1)}), bf16[16,2,32,256]{3,1,2,0:T(2,128)(2,1)S(1)}, u32[]{:S(2)}, u32[]{:S(2)}) async-start(bf16[16,2,32,256]{3,1,2,0:T(2,128)(2,1)} %copy.57), calls=%async_computation | async-start | bytes 1048576 | tf_op jit(solution)/shard_map/all_to_all | solution.py:43
  25.2 3.0 reshape.439
  30.6 3.0 reshape.440
  33.8 8.7 %all-to-all-done = bf16[16,2,32,256]{3,1,2,0:T(2,128)(2,1)S(1)} async-done(((bf16[16,2,32,256]{3,1,2,0:T(2,128)(2,1)}), bf16[16,2,32,256]{3,1,2,0:T(2,128)(2,1)S(1)}, u32[]{:S(2)}, u32[]{:S(2)}) %all-to-all-start) | async-done | bytes 524320 | tf_op jit(solution)/shard_map/all_to_all | solution.py:43
  43.9 11.2 %all-to-all-start.1 = ((bf16[16,2,32,256]{3,1,0,2:T(2,128)(2,1)}), bf16[16,2,32,256]{3,1,0,2:T(2,128)(2,1)S(1)}, u32[]{:S(2)}, u32[]{:S(2)}) async-start(bf16[16,2,32,256]{3,1,0,2:T(2,128)(2,1)} %copy.58), calls=%async_computation.1 | async-start | bytes 1048576 | tf_op jit(solution)/shard_map/all_to_all | solution.py:42
  55.5 30.4 %scatter_custom_fusion.1 = s32[1025]{0:T(1024)S(1)} fusion(s32[8192]{0:T(1024)S(1)} %bitcast.35, s32[8192]{0:T(1024)S(1)} %reshape.505, s32[]{:T(128)} %constant.137.clone.1), kind=kCustom, calls=%fused_computation.76 | custom fusion | bytes 4104 | tf_op jit(solution)/shard_map/scatter | solution.py:63
  86.3 4.9 %gather_fusion.3 = bf16[1024,256]{1,0:T(8,128)(2,1)} fusion(bf16[1025,256]{1,0:T(8,128)(2,1)S(1)} %concatenate.10, s32[1024]{0:T(1024)S(1)} %fusion.23), kind=kCustom, calls=%fused_computation.clone | custom fusion | bytes 1052672 | tf_op jit(solution)/shard_map/jit(_take)/gather | solution.py:76
  94.8 2.7 reshape.441
  97.5 2.7 reshape.442
  100.3 30.4 %scatter_custom_fusion = s32[1025]{0:T(1024)S(1)} fusion(s32[8192]{0:T(1024)S(1)} %bitcast.34, s32[8192]{0:T(1024)S(1)} %fusion.7, s32[]{:T(128)} %constant.137.clone.1), kind=kCustom, calls=%fused_computation.78 | custom fusion | bytes 4104 | tf_op jit(solution)/shard_map/scatter | solution.py:68
  135.3 30.4 %scatter_custom_fusion.2 = f32[1025]{0:T(1024)S(1)} fusion(s32[8192]{0:T(1024)S(1)} %bitcast.36, f32[8192]{0:T(1024)S(1)} %reshape.513, f32[]{:T(128)} %constant.147.clone.1), kind=kCustom, calls=%fused_computation.67 | custom fusion | bytes 4104 | tf_op jit(solution)/shard_map/scatter | solution.py:73
  165.8 81.4 %all-reduce.4.cloned.1.call-done = bf16[8,128,512]{2,1,0:T(8,128)(2,1)} async-done(((bf16[8,128,512]{2,1,0:T(8,128)(2,1)}), bf16[8,128,512]{2,1,0:T(8,128)(2,1)}) %all-reduce.4.cloned.1.call-update) | async-done | bytes 1048592 | tf_op jit(solution)/shard_map/psum | solution.py:81
  247.2 3.4 fusion.29
  250.6 6.8 %gather_fusion = bf16[1024]{0:T(1024)(128)(2,1)S(1)} fusion(bf16[1025]{0:T(1024)(128)(2,1)S(1)} %pad_maximum_fusion, s32[1024]{0:T(1024)S(1)} %get-tuple-element.34), kind=kCustom, calls=%fused_computation.2 | custom fusion | bytes 8192 | tf_op jit(solution)/shard_map/jit(_take)/gather | solution.py:112
  258.1 12.0 %all-to-all-start.2 = ((bf16[16,2,32]{2,1,0:T(2,128)(2,1)}), bf16[16,2,32]{2,1,0:T(2,128)(2,1)S(1)}, u32[]{:S(2)}, u32[]{:S(2)}) async-start(bf16[16,2,32]{2,1,0:T(2,128)(2,1)} %and_select_fusion.2), calls=%async_computation.2 | async-start | bytes 16384 | tf_op jit(solution)/shard_map/all_to_all | solution.py:115
  272.5 5.0 %gather_fusion.4 = bf16[1024,256]{1,0:T(8,128)(2,1)} fusion(bf16[1025,256]{1,0:T(8,128)(2,1)S(1)} %concatenate.12, s32[1024]{0:T(1024)S(1)} %get-tuple-element.34), kind=kCustom, calls=%fused_computation.1.clone | custom fusion | bytes 1052672 | tf_op jit(solution)/shard_map/jit(_take)/gather | solution.py:109
  279.5 7.2 %all-to-all-start.3 = ((bf16[16,2,32,256]{3,2,1,0:T(8,128)(2,1)}), bf16[16,2,32,256]{3,2,1,0:T(8,128)(2,1)S(1)}, u32[]{:S(2)}, u32[]{:S(2)}) async-start(bf16[16,2,32,256]{3,2,1,0:T(8,128)(2,1)} %bitcast.29), calls=%async_computation.3 | async-start | bytes 1048576 | tf_op jit(solution)/shard_map/all_to_all | solution.py:114
  287.5 3.5 gather_fusion.1
  291.2 12.8 %all-to-all-done.3 = bf16[16,2,32,256]{3,2,1,0:T(8,128)(2,1)S(1)} async-done(((bf16[16,2,32,256]{3,2,1,0:T(8,128)(2,1)}), bf16[16,2,32,256]{3,2,1,0:T(8,128)(2,1)S(1)}, u32[]{:S(2)}, u32[]{:S(2)}) %all-to-all-start.3) | async-done | bytes 524320 | tf_op jit(solution)/shard_map/all_to_all | solution.py:114
  308.1 29.1 %all-gather.2.cloned.1.call-done = bf16[256,8192]{1,0:T(8,128)(2,1)} async-done(((bf16[8,8192]{1,0:T(8,128)(2,1)}), bf16[256,8192]{1,0:T(8,128)(2,1)}) %all-gather.2.cloned.1.call-update) | async-done | bytes 4194320 | tf_op jit(solution)/shard_map/all_gather | solution.py:130
  337.3 5.4 %convolution_convert_fusion = bf16[256,8192]{1,0:T(8,128)(2,1)} fusion(bf16[256,256]{1,0:T(8,128)(2,1)S(1)} %fusion.3, bf16[256,8192]{1,0:T(8,128)(2,1)} %all-gather.2.cloned.1.call-done), kind=kOutput, calls=%fused_computation.8 | convolution fusion | flops 1075838976 | bytes 8519680 | tf_op jit(solution)/shard_map/dot_general | solution.py:128
  342.7 3.8 convolution_convert_fusion.2
  347.2 58.5 %reduce-scatter.2.cloned.1.call-done = bf16[256,512]{1,0:T(8,128)(2,1)} async-done(((bf16[256,8192]{1,0:T(8,128)(2,1)}), bf16[256,512]{1,0:T(8,128)(2,1)}) %reduce-scatter.2.cloned.1.call-update) | async-done | bytes 262160 | tf_op jit(solution)/shard_map/reduce_scatter | solution.py:134
  (73 shorter events, 28.0 us)
Async XLA Ops:
  7.2 85.4 %copy-start = (bf16[8,256,512]{2,1,0:T(8,128)(2,1)S(1)}, bf16[8,256,512]{2,1,0:T(8,128)(2,1)}, u32[]{:S(2)}) copy-start(bf16[8,256,512]{2,1,0:T(8,128)(2,1)} %param.15) | copy-start | bytes 6291460
  7.2 5.8 %copy-start.1 = (bf16[8,8192]{1,0:T(8,128)(2,1)S(1)}, bf16[8,8192]{1,0:T(8,128)(2,1)}, u32[]{:S(2)}) copy-start(bf16[8,8192]{1,0:T(8,128)(2,1)} %param.10) | copy-start | bytes 393220
  14.8 13.7 %copy-start.2 = (s32[4096,2]{0,1:T(2,128)S(1)}, s32[4096,2]{0,1:T(2,128)}, u32[]{:S(2)}) copy-start(s32[4096,2]{0,1:T(2,128)} %param.13) | copy-start | bytes 98308
  14.8 27.7 %all-to-all-start = ((bf16[16,2,32,256]{3,1,2,0:T(2,128)(2,1)}), bf16[16,2,32,256]{3,1,2,0:T(2,128)(2,1)S(1)}, u32[]{:S(2)}, u32[]{:S(2)}) async-start(bf16[16,2,32,256]{3,1,2,0:T(2,128)(2,1)} %copy.57), calls=%async_computation | async-start | bytes 1048576 | tf_op jit(solution)/shard_map/all_to_all | solution.py:43
  43.9 42.1 %all-to-all-start.1 = ((bf16[16,2,32,256]{3,1,0,2:T(2,128)(2,1)}), bf16[16,2,32,256]{3,1,0,2:T(2,128)(2,1)S(1)}, u32[]{:S(2)}, u32[]{:S(2)}) async-start(bf16[16,2,32,256]{3,1,0,2:T(2,128)(2,1)} %copy.58), calls=%async_computation.1 | async-start | bytes 1048576 | tf_op jit(solution)/shard_map/all_to_all | solution.py:42
  55.1 192.1 %all-reduce.4.cloned.1.call-start = ((), (), s32[]{:S(2)}) async-start(), calls=%async_computation.5 | async-start | bytes 2097152 | tf_op jit(solution)/shard_map/psum | solution.py:81
  94.0 243.2 %all-gather.2.cloned.1.call-start = ((), (), s32[]{:S(2)}) async-start(), calls=%async_computation.6 | async-start | bytes 4325376 | tf_op jit(solution)/shard_map/all_gather | solution.py:130
  94.8 36.1 %copy-start.3 = (bf16[4096,2]{0,1:T(2,128)(2,1)S(1)}, bf16[4096,2]{0,1:T(2,128)(2,1)}, u32[]{:S(2)}) copy-start(bf16[4096,2]{0,1:T(2,128)(2,1)} %param.14) | copy-start | bytes 49156
  130.8 116.4 %copy-start.4 = (f32[8,512]{1,0:T(8,128)S(1)}, f32[8,512]{1,0:T(8,128)}, u32[]{:S(2)}) copy-start(f32[8,512]{1,0:T(8,128)} %param.16) | copy-start | bytes 49156
  130.9 116.4 %copy-start.5 = (f32[8,512]{1,0:T(8,128)S(1)}, f32[8,512]{1,0:T(8,128)}, u32[]{:S(2)}) copy-start(f32[8,512]{1,0:T(8,128)} %param.17) | copy-start | bytes 49156
  258.1 21.4 %all-to-all-start.2 = ((bf16[16,2,32]{2,1,0:T(2,128)(2,1)}), bf16[16,2,32]{2,1,0:T(2,128)(2,1)S(1)}, u32[]{:S(2)}, u32[]{:S(2)}) async-start(bf16[16,2,32]{2,1,0:T(2,128)(2,1)} %and_select_fusion.2), calls=%async_computation.2 | async-start | bytes 16384 | tf_op jit(solution)/shard_map/all_to_all | solution.py:115
  279.5 24.5 %all-to-all-start.3 = ((bf16[16,2,32,256]{3,2,1,0:T(8,128)(2,1)}), bf16[16,2,32,256]{3,2,1,0:T(8,128)(2,1)S(1)}, u32[]{:S(2)}, u32[]{:S(2)}) async-start(bf16[16,2,32,256]{3,2,1,0:T(8,128)(2,1)} %bitcast.29), calls=%async_computation.3 | async-start | bytes 1048576 | tf_op jit(solution)/shard_map/all_to_all | solution.py:114
  286.8 119.0 %reduce-scatter.2.cloned.1.call-start = ((), (), s32[]{:S(2)}) async-start(), calls=%async_computation.7 | async-start | bytes 4456448 | tf_op jit(solution)/shard_map/reduce_scatter | solution.py:134
Sparse Core Ops, SparseCore 0:
  94.2 153.0 all-reduce.3
  250.4 86.8 all-gather.1
  342.8 62.8 reduce-scatter.1
where the time goes:
time: 414 us; the launch traced here: 412 us
  waiting for transfers between devices  191 us (46%)
  local copies, waits for them, and re-layouts  142 us (34%)
  starting transfers between devices  41.3 us (10%)
  between operations  14.1 us (3%)
  matrix products  13.4 us (3%)
  other arithmetic  10.4 us (3%)
    psum x1, waiting for transfers between devices, local(): lax.psum(partial_pre.astype(jnp.bfloat16), 'rule').astype(jnp.float32)  81.4 us
    reduce_scatter x1, waiting for transfers between devices, local(): lax.psum_scatter(group_term.astype(jnp.bfloat16), 'dp', scatter_dimension...  58.5 us
    scatter x1, local copies, waits for them, and re-layouts, local(): to_recv = jnp.full((buffer_rows + 1,), recv_count, jnp.int32).at[pos_targ...  30.4 us
    scatter x1, local copies, waits for them, and re-layouts, local(): to_buffer = jnp.full((recv_count + 1,), buffer_rows, jnp.int32).at[recv_t...  30.4 us
    scatter x1, local copies, waits for them, and re-layouts, local(): cot_buffer = jnp.zeros((buffer_rows + 1,), jnp.float32).at[pos_target].se...  30.4 us
    all_gather x1, waiting for transfers between devices, local(): lax.all_gather(attn_input, 'rule', axis=0, tiled=True)  29.1 us
    all_to_all x1, waiting for transfers between devices, local(): lax.all_to_all(back_rows, 'dp', split_axis=0, concat_axis=0, tiled=True)  12.8 us
    all_to_all x1, starting transfers between devices, local(): lax.all_to_all(back_reward, 'dp', split_axis=0, concat_axis=0, tiled=True)  12 us
  transfers between devices with their start and end apart: 7, of which 5 were waited for; matrix products, arithmetic and copies ran while one was open for 35% of the time, Pallas kernels for 0%

commit v1 on v0

v1 whole, which is shorter than its diff:
```python
import functools

import jax
import jax.numpy as jnp
from jax import lax
from jax.experimental import pallas as pl
from jax.experimental.pallas import tpu as pltpu
from jax.sharding import PartitionSpec as P

BF16 = jnp.bfloat16
F32 = jnp.float32
NN = (((1,), (0,)), ((), ()))
NT = (((1,), (1,)), ((), ()))
TN = (((0,), (0,)), ((), ()))


def mm(a, b, dims=NN):
    return lax.dot_general(a, b, dims, preferred_element_type=F32)


def tables_kernel(block, me_ref, owner_ref, pos_ref, cot_ref, sort_ref, unsort_ref, pick_ref, cot_out_ref):
    me = me_ref[0]
    groups, tokens = owner_ref.shape[1:]
    rows = sort_ref.shape[0]
    slots = 2 * (tokens // block)
    owner = [owner_ref[k] for k in range(2)]
    pos = [pos_ref[k] for k in range(2)]
    cot = [cot_ref[k].astype(F32) for k in range(2)]
    token = lax.broadcasted_iota(jnp.int32, (groups, tokens), 1)
    in_block = token % block
    rank = [jnp.zeros((groups, tokens), jnp.int32), (owner[0] == owner[1]).astype(jnp.int32)]
    for shift in range(1, block):
        for other in range(2):
            moved = pltpu.roll(owner[other], shift, 1)
            for k in range(2):
                hit = (moved == owner[k]) & (in_block >= shift)
                rank[k] = rank[k] + hit.astype(jnp.int32)
    place = [2 * (token // block) + rank[k] for k in range(2)]
    held = [pos[k] >= 0 for k in range(2)]

    mine = lax.broadcasted_iota(jnp.int32, (groups, tokens), 0) == me
    slot_row = lax.broadcasted_iota(jnp.int32, (groups * slots, tokens), 0)
    for k in range(2):
        key = jnp.where(held[k], owner[k] * slots + place[k], -1)
        key = jnp.sum(jnp.where(mine, key, 0), axis=0, keepdims=True)
        pick_ref[k] = jnp.where(slot_row == key, 1.0, 0.0).astype(BF16)

    received = [jnp.where(held[k] & (owner[k] == me), place[k], -1) for k in range(2)]
    high = [((pos[k] + 1) // 32).astype(F32).astype(BF16) for k in range(2)]
    low = [((pos[k] + 1) % 32).astype(F32).astype(BF16) for k in range(2)]
    cot = [cot[k].astype(BF16) for k in range(2)]
    pair = 128 // slots
    cot_total = jnp.zeros((rows, 128), F32)
    lane_row = lax.broadcasted_iota(jnp.int32, (128, tokens), 0)
    buffer_row = lax.broadcasted_iota(jnp.int32, (rows, 128), 0)
    buffer_lane = lax.broadcasted_iota(jnp.int32, (128, rows), 1)
    for step in range(groups // pair):
        ones, highs, lows, cots = [], [], [], []
        for part in range(pair):
            g = step * pair + part
            for k in range(2):
                row = received[k][g : g + 1]
                row = jnp.where(row >= 0, row + part * slots, -1)
                ones.append(jnp.where(lane_row == row, 1.0, 0.0).astype(BF16))
                highs.append(high[k][g : g + 1])
                lows.append(low[k][g : g + 1])
                cots.append(cot[k][g : g + 1])
        chosen = jnp.concatenate(ones, axis=1)
        wide = chosen.shape[1]
        high_row = jnp.broadcast_to(jnp.concatenate(highs, axis=1), (128, wide))
        low_row = jnp.broadcast_to(jnp.concatenate(lows, axis=1), (128, wide))
        cot_row = jnp.broadcast_to(jnp.concatenate(cots, axis=1), (128, wide))
        at_lane = (mm(high_row, chosen, NT) * 32.0 + mm(low_row, chosen, NT)).astype(jnp.int32) - 1
        at_row = (mm(chosen, high_row, NT) * 32.0 + mm(chosen, low_row, NT)).astype(jnp.int32) - 1
        cot_lane = mm(cot_row, chosen, NT).astype(BF16)
        hit = jnp.where(buffer_row == at_lane[0:1], 1.0, 0.0).astype(BF16)
        sort_ref[:, step * 128 : (step + 1) * 128] = hit
        cot_total = cot_total + mm(hit, cot_lane, NT)
        at_row = jnp.concatenate([at_row] * (rows // 128), axis=1)
        unsort_ref[step * 128 : (step + 1) * 128, :] = jnp.where(buffer_lane == at_row, 1.0, 0.0).astype(BF16)
    cot_out_ref[...] = cot_total


def tables(block, rows, me, owner, pos, cot):
    groups, tokens = owner.shape[1:]
    received = groups * 2 * (tokens // block)
    vmem = pl.BlockSpec(memory_space=pltpu.VMEM)
    return pl.pallas_call(
        functools.partial(tables_kernel, block),
        out_shape=(
            jax.ShapeDtypeStruct((rows, received), BF16),
            jax.ShapeDtypeStruct((received, rows), BF16),
            jax.ShapeDtypeStruct((2, received, tokens), BF16),
            jax.ShapeDtypeStruct((rows, 128), F32),
        ),
        in_specs=[pl.BlockSpec(memory_space=pltpu.SMEM), vmem, vmem, vmem],
        out_specs=(vmem, vmem, vmem, vmem),
        compiler_params=pltpu.CompilerParams(vmem_limit_bytes=32 * 2**20),
        cost_estimate=pl.CostEstimate(flops=10**9, bytes_accessed=6 * 2**20, transcendentals=0),
    )(me, owner, pos, cot)


def forward_kernel(sort_ref, got_ref, weight_ref, rows_ref, part_ref):
    rows = mm(sort_ref[...], got_ref[...]).astype(BF16)
    rows_ref[...] = rows
    part_ref[...] = mm(rows, weight_ref[0]).astype(BF16)


def forward(sort, got, weight):
    adapters, features, hidden = weight.shape
    rows, received = sort.shape
    capacity = rows // adapters
    return pl.pallas_call(
        forward_kernel,
        grid=(adapters,),
        out_shape=(
            jax.ShapeDtypeStruct((rows, features), BF16),
            jax.ShapeDtypeStruct((rows, hidden), BF16),
        ),
        in_specs=[
            pl.BlockSpec((capacity, received), lambda a: (a, 0)),
            pl.BlockSpec((received, features), lambda a: (0, 0)),
            pl.BlockSpec((1, features, hidden), lambda a: (a, 0, 0)),
        ],
        out_specs=(
            pl.BlockSpec((capacity, features), lambda a: (a, 0)),
            pl.BlockSpec((capacity, hidden), lambda a: (a, 0)),
        ),
        compiler_params=pltpu.CompilerParams(vmem_limit_bytes=32 * 2**20),
        cost_estimate=pl.CostEstimate(flops=10**9, bytes_accessed=6 * 2**20, transcendentals=0),
    )(sort, got, weight)


def backward_kernel(
    pre_ref, bias_ref, out_ref, cot_ref, weight_ref, unsort_ref,
    half_ref, bias_grad_ref, out_grad_ref, back_ref, reward_ref, grads,
):
    a = pl.program_id(0)
    capacity, hidden = pre_ref.shape
    features = weight_ref.shape[1]
    read_out = out_ref[0]
    pre = pre_ref[...].astype(F32) + bias_ref[0]
    s = 1.0 / (1.0 + jnp.exp(-pre))
    cot = jnp.concatenate([cot_ref[...]] * (hidden // 128), axis=1)
    activated = pre * s
    grad_pre = cot * read_out * s * (1.0 + pre * (1.0 - s))
    half = grad_pre.astype(BF16)
    half_ref[...] = half
    bias_grad_ref[0] = jnp.sum(grad_pre, axis=0, keepdims=True)
    out_grad_ref[0] = jnp.sum(cot * activated, axis=0, keepdims=True)
    reward = jnp.sum(activated * read_out, axis=1, keepdims=True)
    at = pl.ds(pl.multiple_of(a * capacity, capacity), capacity)
    grads[at, :features] = mm(half, weight_ref[0], NT).astype(BF16)
    grads[at, features:] = jnp.broadcast_to(reward, (capacity, 128)).astype(BF16)

    @pl.when(a == pl.num_programs(0) - 1)
    def _():
        back = mm(unsort_ref[...], grads[...]).astype(BF16)
        back_ref[...] = back[:, :features]
        first = lax.broadcasted_iota(jnp.int32, (16, 128), 1) == 0
        first = jnp.where(first, 1.0, 0.0).astype(BF16)
        reward_ref[...] = mm(first, back[:, features:], NT).astype(BF16)


def backward(pre, bias, read_out, cot, weight, unsort):
    adapters, features, hidden = weight.shape
    received, rows = unsort.shape
    capacity = rows // adapters
    line = pl.BlockSpec((1, 1, hidden), lambda a: (a, 0, 0))
    half, bias_grad, out_grad, back, reward = pl.pallas_call(
        backward_kernel,
        grid=(adapters,),
        out_shape=(
            jax.ShapeDtypeStruct((rows, hidden), BF16),
            jax.ShapeDtypeStruct((adapters, 1, hidden), F32),
            jax.ShapeDtypeStruct((adapters, 1, hidden), F32),
            jax.ShapeDtypeStruct((received, features), BF16),
            jax.ShapeDtypeStruct((16, received), BF16),
        ),
        in_specs=[
            pl.BlockSpec((capacity, hidden), lambda a: (a, 0)),
            line,
            line,
            pl.BlockSpec((capacity, 128), lambda a: (a, 0)),
            pl.BlockSpec((1, features, hidden), lambda a: (a, 0, 0)),
            pl.BlockSpec((received, rows), lambda a: (0, 0)),
        ],
        out_specs=(
            pl.BlockSpec((capacity, hidden), lambda a: (a, 0)),
            line,
            line,
            pl.BlockSpec((received, features), lambda a: (0, 0)),
            pl.BlockSpec((16, received), lambda a: (0, 0)),
        ),
        scratch_shapes=[pltpu.VMEM((rows, features + 128), BF16)],
        compiler_params=pltpu.CompilerParams(vmem_limit_bytes=32 * 2**20),
        cost_estimate=pl.CostEstimate(flops=10**9, bytes_accessed=8 * 2**20, transcendentals=2**19),
    )(pre, bias[:, None], read_out[:, None], cot, weight, unsort)
    return half, bias_grad[:, 0], out_grad[:, 0], back, reward


def local(
    hidden_states, attn_input, rule_ids, slot_ids, cotangent, adapter_in, adapter_bias, adapter_out
):
    dp_size = lax.axis_size("dp")
    rule_size = lax.axis_size("rule")
    block = hidden_states.shape[0]
    adapters, feature_cols, hidden_units = adapter_in.shape
    tokens = block * rule_size
    capacity = 4 * block * rule_size // adapters
    rows = adapters * capacity
    slots = 2 * rule_size

    group_rows = lax.all_to_all(hidden_states, "rule", split_axis=1, concat_axis=0, tiled=True)
    attn_cols = lax.all_to_all(attn_input, "dp", split_axis=1, concat_axis=0, tiled=True)
    attn_all = lax.all_gather(
        attn_cols.reshape(dp_size, block, -1), "rule", axis=1, tiled=True
    ).reshape(dp_size * tokens, -1)

    rule_all = rule_ids.T.reshape(2, dp_size, tokens)
    slot_all = slot_ids.T.reshape(2, dp_size, tokens)
    cot_all = cotangent.T.reshape(2, dp_size, tokens)
    owner = rule_all // adapters
    pos = jnp.where(slot_all >= 0, rule_all % adapters * capacity + slot_all, -1)
    me = lax.axis_index("dp").astype(jnp.int32).reshape(1)
    sort, unsort, pick, cot_rows = tables(block, rows, me, owner, pos, cot_all)
    pick_sum = pick[0] + pick[1]

    outgoing = mm(pick_sum, group_rows).astype(BF16)
    got = lax.all_to_all(outgoing, "dp", split_axis=0, concat_axis=0, tiled=True)
    rows_buf, partial_pre = forward(sort, got, adapter_in)
    shares = lax.all_to_all(partial_pre, "rule", split_axis=0, concat_axis=0, tiled=True)
    share = jnp.sum(
        shares.reshape(rule_size, rows // rule_size, hidden_units).astype(F32), axis=0
    ).astype(BF16)
    share = jnp.broadcast_to(share[None], (rule_size,) + share.shape).reshape(rows, hidden_units)
    preact = lax.all_to_all(share, "rule", split_axis=0, concat_axis=0, tiled=True)

    grad_half, bias_grad, out_grad, back, reward = backward(
        preact, adapter_bias, adapter_out, cot_rows, adapter_in, unsort
    )
    returned = lax.all_to_all(back, "dp", split_axis=0, concat_axis=0, tiled=True)
    state_grad = mm(pick_sum, returned, TN).astype(BF16)
    state_all = lax.all_gather(state_grad, "dp", axis=0, tiled=True)

    reward_back = lax.all_to_all(
        reward[0].reshape(dp_size, slots), "dp", split_axis=0, concat_axis=0, tiled=True
    )
    rewards = lax.dot_general(
        pick, reward_back.reshape(-1), (((1,), (0,)), ((), ())), preferred_element_type=F32
    )
    rewards = rewards.astype(BF16).T
    in_grad = jnp.einsum(
        "acd,acr->adr",
        rows_buf.reshape(adapters, capacity, feature_cols),
        grad_half.reshape(adapters, capacity, hidden_units),
        preferred_element_type=F32,
    ).astype(BF16)
    o_proj_grad = mm(state_all, attn_all, TN).astype(BF16)
    return (rewards, in_grad, bias_grad, out_grad, o_proj_grad)


def solution(mesh):
    placed = (
        P(("dp", "rule"), None),
        P(("dp", "rule"), None),
        P(),
        P(),
        P(),
        P("dp", "rule", None),
        P("dp", None),
        P("dp", None),
    )
    return jax.shard_map(
        local,
        mesh=mesh,
        in_specs=placed,
        out_specs=(
            P("dp", None),
            P("dp", "rule", None),
            P("dp", None),
            P("dp", None),
            P("rule", "dp"),
        ),
        check_vma=False,
    )
```

time: 414 us -> 235 us (0.57)
  waiting for transfers between devices: 191 us -> 55.4 us
  local copies, waits for them, and re-layouts: 142 us -> 13.3 us
  blocking collectives: 0 us -> 109 us
  starting transfers between devices: 41.3 us -> 22.2 us
  Pallas kernels: 0 us -> 11.5 us
  other arithmetic: 10.4 us -> 1.01 us
  matrix products: 13.4 us -> 8.46 us
    all_to_all x0 -> x4, blocking collectives: none -> 109 us  [the longest x1 41.1 us: local(): lax.all_to_all(partial_pre, 'rule', split_axis=0, concat_axis=0, tiled=True)]
    scatter x3 -> x0, local copies, waits for them, and re-layouts: 91.3 us -> none  [the longest x1 30.4 us: local(): to_recv = jnp.full((buffer_rows + 1,), recv_count, jnp.int32).at[pos_targ...]
    psum x1 -> x0, waiting for transfers between devices: 81.4 us -> none  [local(): lax.psum(partial_pre.astype(jnp.bfloat16), 'rule').astype(jnp.float32)]
    reduce_scatter x1 -> x0, waiting for transfers between devices: 58.5 us -> none  [local(): lax.psum_scatter(group_term.astype(jnp.bfloat16), 'dp', scatter_dimension...]
    gather x8 -> x0, local copies, waits for them, and re-layouts: 22.5 us -> none  [the longest x2 6.87 us: local(): jnp.take(reward_flat, to_buffer, axis=0)]
    all_to_all x4 -> x3, starting transfers between devices: 40.8 us -> 22.1 us  [the longest x1 10.7 us: local(): lax.all_to_all(hidden_states, 'rule', split_axis=1, concat_axis=0, tiled=...]
    reshape x10 -> x1, local copies, waits for them, and re-layouts: 15.4 us -> 0.09 us  [local(): reward_back.reshape(-1)]
    pallas_call x0 -> x3, Pallas kernels: none -> 11.5 us  [the longest x1 4.43 us: tables(): pl.pallas_call(functools.partial(tables_kernel, block), out_shape=(jax.Sh...]
  transfers between devices with their start and end apart: 7 -> 5, of which waited for: 5 -> 3; matrix products, arithmetic and copies ran while one was open for 35% -> 3% of each run, Pallas kernels for 0% -> 5%
where the time goes in v1:
time: 235 us
  blocking collectives  109 us (46%)
  waiting for transfers between devices  55.4 us (24%)
  starting transfers between devices  22.2 us (9%)
  between operations  14.2 us (6%)
  local copies, waits for them, and re-layouts  13.3 us (6%)
  Pallas kernels  11.5 us (5%)
  matrix products  8.46 us (4%)
    all_to_all x1, blocking collectives, local(): lax.all_to_all(partial_pre, 'rule', split_axis=0, concat_axis=0, tiled=True)  41.1 us
    all_to_all x1, waiting for transfers between devices, local(): lax.all_to_all(share, 'rule', split_axis=0, concat_axis=0, tiled=True)  28.5 us
    all_to_all x1, blocking collectives, local(): lax.all_to_all(back, 'dp', split_axis=0, concat_axis=0, tiled=True)  26.2 us
    all_gather x1, waiting for transfers between devices, local(): state_all = lax.all_gather(state_grad, 'dp', axis=0, tiled=True)  22.9 us
    all_to_all x1, blocking collectives, local(): lax.all_to_all(outgoing, 'dp', split_axis=0, concat_axis=0, tiled=True)  21.3 us
    all_to_all x1, blocking collectives, local(): lax.all_to_all(attn_input, 'dp', split_axis=1, concat_axis=0, tiled=True)  20.1 us
    unnamed x34, local copies, waits for them, and re-layouts  10.8 us
    all_to_all x1, starting transfers between devices, local(): lax.all_to_all(hidden_states, 'rule', split_axis=1, concat_axis=0, tiled=...  10.7 us
  transfers between devices with their start and end apart: 5, of which 3 were waited for; matrix products, arithmetic and copies ran while one was open for 3% of the time, Pallas kernels for 5%

profile of v1, /device:TPU:1, one launch (start us, length us, event | category | flops | bytes accessed | tf_op | source)
XLA Modules:
  0.0 234.7 jit_solution(4909523537401098394)
XLA Ops:
  7.2 20.1 %all_to_all.85 = bf16[8,16,512]{2,0,1:T(8,128)(2,1)} all-to-all(bf16[8,16,512]{2,0,1:T(8,128)(2,1)} %bitcast.92), channel_id=1, replica_groups=mesh['dp'=16,'rule'=32] {'dp'}, dimensions={1} | all-to-all | bytes 262144 | tf_op jit(solution)/shard_map/all_to_all | solution.py:215
  27.3 10.7 %all-to-all-start = ((bf16[8,32,256]{2,0,1:T(8,128)(2,1)}), bf16[8,32,256]{2,0,1:T(8,128)(2,1)S(1)}, u32[]{:S(2)}, u32[]{:S(2)}) async-start(bf16[8,32,256]{2,0,1:T(8,128)(2,1)} %bitcast.93), calls=%async_computation | async-start | bytes 262144 | tf_op jit(solution)/shard_map/all_to_all | solution.py:214
  39.6 4.4 %shard_map.119 = (bf16[1024,1024]{1,0:T(8,128)(2,1)S(1)}, bf16[1024,1024]{1,0:T(8,128)(2,1)S(1)}, bf16[2,1024,256]{2,1,0:T(8,128)(2,1)S(1)}, f32[1024,128]{1,0:T(8,128)S(1)}) custom-call(s32[1]{0:T(128)} %bitcast.me_ref, s32[2,16,256]{2,1,0:T(8,128)S(1)} %get-tuple-element.28.owner_ref, s32[2,16,256]{2,1,0:T(8,128)S(1)} %get-tuple-element.27.pos_ref, ...), custom_call_target="tpu_custom_call" | custom-call | flops 1000000000 | bytes 6291456 | tf_op jit(solution)/shard_map/pallas_call | solution.py:88
  44.0 1.3 copy-done.1
  45.3 1.3 copy-done.3
  46.7 0.8 copy-done.12
  47.8 21.3 %all_to_all.86 = bf16[16,64,256]{2,1,0:T(8,128)(2,1)S(1)} all-to-all(bf16[16,64,256]{2,1,0:T(8,128)(2,1)S(1)} %bitcast.89), channel_id=1, replica_groups=mesh['dp'=16,'rule'=32] {'dp'}, dimensions={0} | all-to-all | bytes 1048576 | tf_op jit(solution)/shard_map/all_to_all | solution.py:230
  69.2 1.6 copy-done.2
  70.8 3.4 %shard_map.120 = (bf16[1024,256]{1,0:T(8,128)(2,1)S(1)}, bf16[1024,512]{1,0:T(8,128)(2,1)S(1)}) custom-call(bf16[1024,1024]{1,0:T(8,128)(2,1)S(1)} %copy-done.2, bf16[1024,256]{1,0:T(8,128)(2,1)S(1)} %bitcast.83, bf16[8,256,512]{2,1,0:T(8,128)(2,1)S(1)} %copy-done), custom_call_target="tpu_custom_call" | custom-call | flops 1000000000 | bytes 6291456 | tf_op jit(solution)/shard_map/pallas_call | solution.py:113
  74.9 41.1 %all_to_all.87 = bf16[32,32,512]{2,1,0:T(8,128)(2,1)S(1)} all-to-all(bf16[32,32,512]{2,1,0:T(8,128)(2,1)S(1)} %bitcast.85), channel_id=1, replica_groups=mesh['dp'=16,'rule'=32] {'rule'}, dimensions={0} | all-to-all | bytes 2097152 | tf_op jit(solution)/shard_map/all_to_all | solution.py:232
  116.2 1.1 broadcast_in_dim.14
  117.3 8.1 %all-to-all-start.3 = ((bf16[32,32,512]{2,1,0:T(8,128)(2,1)}), bf16[32,32,512]{2,1,0:T(8,128)(2,1)S(1)}, u32[]{:S(2)}, u32[]{:S(2)}) async-start(bf16[32,32,512]{2,1,0:T(8,128)(2,1)} %broadcast_in_dim.14), calls=%async_computation.3 | async-start | bytes 2097152 | tf_op jit(solution)/shard_map/all_to_all | solution.py:237
  125.5 28.5 %all-to-all-done.3 = bf16[32,32,512]{2,1,0:T(8,128)(2,1)S(1)} async-done(((bf16[32,32,512]{2,1,0:T(8,128)(2,1)}), bf16[32,32,512]{2,1,0:T(8,128)(2,1)S(1)}, u32[]{:S(2)}, u32[]{:S(2)}) %all-to-all-start.3) | async-done | bytes 1048608 | tf_op jit(solution)/shard_map/all_to_all | solution.py:237
  154.0 1.6 copy-done.4
  155.6 1.0 copy-done.13
  156.7 3.7 %shard_map.121 = (bf16[1024,512]{1,0:T(8,128)(2,1)S(1)}, f32[8,1,512]{2,1,0:T(1,128)S(1)}, f32[8,1,512]{2,1,0:T(1,128)S(1)}, bf16[1024,256]{1,0:T(8,128)(2,1)S(1)}, bf16[16,1024]{1,0:T(8,128)(2,1)S(1)}) custom-call(bf16[1024,512]{1,0:T(8,128)(2,1)S(1)} %bitcast.82, f32[8,1,512]{2,1,0:T(1,128)S(1)} %broadcast_in_dim.15.bias_ref, ...), custom_call_target="tpu_custom_call" | custom-call | flops 1000000000 | bytes 8388608 | tf_op jit(solution)/shard_map/pallas_call | solution.py:170
  160.4 1.0 copy-done.5
  161.3 26.2 %all_to_all.88 = bf16[16,64,256]{2,1,0:T(8,128)(2,1)S(1)} all-to-all(bf16[16,64,256]{2,1,0:T(8,128)(2,1)S(1)} %bitcast.87), channel_id=1, replica_groups=mesh['dp'=16,'rule'=32] {'dp'}, dimensions={0} | all-to-all | bytes 1048576 | tf_op jit(solution)/shard_map/all_to_all | solution.py:242
  187.5 1.1 convolution_convert_fusion.3
  189.3 3.3 %all-to-all-start.4 = ((bf16[16,1,64]{2,1,0:T(2,128)(2,1)}), bf16[16,1,64]{2,1,0:T(2,128)(2,1)S(1)}, u32[]{:S(2)}, u32[]{:S(2)}) async-start(bf16[16,1,64]{2,1,0:T(2,128)(2,1)} %all_to_all.77), calls=%async_computation.4 | async-start | bytes 16384 | tf_op jit(solution)/shard_map/all_to_all | solution.py:246
  192.6 2.1 convolution_convert_fusion
  195.3 4.0 %all-to-all-done.4 = bf16[16,1,64]{2,1,0:T(2,128)(2,1)S(1)} async-done(((bf16[16,1,64]{2,1,0:T(2,128)(2,1)}), bf16[16,1,64]{2,1,0:T(2,128)(2,1)S(1)}, u32[]{:S(2)}, u32[]{:S(2)}) %all-to-all-start.4) | async-done | bytes 2080 | tf_op jit(solution)/shard_map/all_to_all | solution.py:246
  200.2 22.9 %all-gather.3.cloned.1.call-done = bf16[4096,256]{1,0:T(8,128)(2,1)} async-done(((bf16[256,256]{1,0:T(8,128)(2,1)}), bf16[4096,256]{1,0:T(8,128)(2,1)}) %all-gather.3.cloned.1.call-update) | async-done | bytes 2097168 | tf_op jit(solution)/shard_map/all_gather | solution.py:244
  223.1 4.8 %convolution_convert_fusion.2 = bf16[256,512]{1,0:T(8,128)(2,1)} fusion(bf16[4096,256]{1,0:T(8,128)(2,1)} %all-gather.3.cloned.1.call-done, bf16[4096,512]{1,0:T(8,128)(2,1)} %bitcast.98), kind=kOutput, calls=%fused_computation.2 | convolution fusion | flops 1073872896 | bytes 6553600 | tf_op jit(solution)/shard_map/dot_general | solution.py:18
  (44 shorter events, 5.2 us)
Async XLA Ops:
  7.2 193.0 %all-gather.5.cloned.1.call-start = ((), (), s32[]{:S(2)}) async-start(), calls=%async_computation.8 | async-start | bytes 4325376 | tf_op jit(solution)/shard_map/all_gather | solution.py:216
  27.3 20.2 %all-to-all-start = ((bf16[8,32,256]{2,0,1:T(8,128)(2,1)}), bf16[8,32,256]{2,0,1:T(8,128)(2,1)S(1)}, u32[]{:S(2)}, u32[]{:S(2)}) async-start(bf16[8,32,256]{2,0,1:T(8,128)(2,1)} %bitcast.93), calls=%async_computation | async-start | bytes 262144 | tf_op jit(solution)/shard_map/all_to_all | solution.py:214
  44.0 1.3 copy-start.1
  45.3 1.3 copy-start.3
  46.7 0.8 copy-start.12
  47.5 26.6 %copy-start.7 = (bf16[2,1024,256]{2,1,0:T(8,128)(2,1)}, bf16[2,1024,256]{2,1,0:T(8,128)(2,1)S(1)}, u32[]{:S(2)}) copy-start(bf16[2,1024,256]{2,1,0:T(8,128)(2,1)S(1)} %get-tuple-element.16) | copy-start | bytes 3145732
  47.5 21.6 %copy-start = (bf16[8,256,512]{2,1,0:T(8,128)(2,1)S(1)}, bf16[8,256,512]{2,1,0:T(8,128)(2,1)}, u32[]{:S(2)}) copy-start(bf16[8,256,512]{2,1,0:T(8,128)(2,1)} %weight_ref.3) | copy-start | bytes 6291460
  69.2 1.6 copy-start.2
  74.1 0.8 copy-start.10
  116.1 9.4 %copy-start.14 = (f32[8,512]{1,0:T(8,128)S(1)}, f32[8,512]{1,0:T(8,128)}, u32[]{:S(2)}) copy-start(f32[8,512]{1,0:T(8,128)} %param.14) | copy-start | bytes 49156
  116.1 9.4 %copy-start.15 = (f32[8,512]{1,0:T(8,128)S(1)}, f32[8,512]{1,0:T(8,128)}, u32[]{:S(2)}) copy-start(f32[8,512]{1,0:T(8,128)} %param.15) | copy-start | bytes 49156
  117.3 36.7 %all-to-all-start.3 = ((bf16[32,32,512]{2,1,0:T(8,128)(2,1)}), bf16[32,32,512]{2,1,0:T(8,128)(2,1)S(1)}, u32[]{:S(2)}, u32[]{:S(2)}) async-start(bf16[32,32,512]{2,1,0:T(8,128)(2,1)} %broadcast_in_dim.14), calls=%async_computation.3 | async-start | bytes 2097152 | tf_op jit(solution)/shard_map/all_to_all | solution.py:237
  125.4 97.7 %all-gather.3.cloned.1.call-start = ((), (), s32[]{:S(2)}) async-start(), calls=%async_computation.7 | async-start | bytes 2228224 | tf_op jit(solution)/shard_map/all_gather | solution.py:244
  154.0 1.6 copy-start.4
  155.6 1.0 copy-start.13
  156.7 30.8 %copy-start.8 = (bf16[2,1024,256]{2,1,0:T(8,128)(2,1)S(1)}, bf16[2,1024,256]{2,1,0:T(8,128)(2,1)}, u32[]{:S(2)}) copy-start(bf16[2,1024,256]{2,1,0:T(8,128)(2,1)} %copy-done.7) | copy-start | bytes 3145732
  160.4 1.0 copy-start.5
  161.3 31.3 %copy-start.11 = (bf16[1024,256]{1,0:T(8,128)(2,1)S(1)}, bf16[1024,256]{1,0:T(8,128)(2,1)}, u32[]{:S(2)}) copy-start(bf16[1024,256]{1,0:T(8,128)(2,1)} %copy-done.10) | copy-start | bytes 1572868
  161.3 31.3 %copy-start.6 = (bf16[1024,512]{1,0:T(8,128)(2,1)S(1)}, bf16[1024,512]{1,0:T(8,128)(2,1)}, u32[]{:S(2)}) copy-start(bf16[1024,512]{1,0:T(8,128)(2,1)} %copy-done.5) | copy-start | bytes 3145732
  188.6 10.8 %copy-start.9 = (bf16[2,1024,256]{2,1,0:T(8,128)(2,1)S(1)}, bf16[2,1024,256]{2,1,0:T(8,128)(2,1)}, u32[]{:S(2)}) copy-start(bf16[2,1024,256]{2,1,0:T(8,128)(2,1)} %copy-done.7) | copy-start | bytes 3145732
  189.3 10.0 %all-to-all-start.4 = ((bf16[16,1,64]{2,1,0:T(2,128)(2,1)}), bf16[16,1,64]{2,1,0:T(2,128)(2,1)S(1)}, u32[]{:S(2)}, u32[]{:S(2)}) async-start(bf16[16,1,64]{2,1,0:T(2,128)(2,1)} %all_to_all.77), calls=%async_computation.4 | async-start | bytes 16384 | tf_op jit(solution)/shard_map/all_to_all | solution.py:246
Sparse Core Ops, SparseCore 0:
  27.4 111.4 all-gather.4
  188.7 34.3 all-gather.2

commit v2 on v1

--- a/solution.py
+++ b/solution.py
@@ -95,38 +95,51 @@
         ),
         in_specs=[pl.BlockSpec(memory_space=pltpu.SMEM), vmem, vmem, vmem],
         out_specs=(vmem, vmem, vmem, vmem),
-        compiler_params=pltpu.CompilerParams(vmem_limit_bytes=32 * 2**20),
+        compiler_params=pltpu.CompilerParams(vmem_limit_bytes=16 * 2**20),
         cost_estimate=pl.CostEstimate(flops=10**9, bytes_accessed=6 * 2**20, transcendentals=0),
     )(me, owner, pos, cot)
 
 
-def forward_kernel(sort_ref, got_ref, weight_ref, rows_ref, part_ref):
-    rows = mm(sort_ref[...], got_ref[...]).astype(BF16)
+def forward_kernel(sort_ref, got_ref, weight_ref, rows_ref, part_ref, attn_ref):
+    groups, height, features = got_ref.shape
+    slots = sort_ref.shape[1] // groups
+    got = got_ref[:, :slots].reshape(groups * slots, features)
+    rows = mm(sort_ref[...], got).astype(BF16)
     rows_ref[...] = rows
     part_ref[...] = mm(rows, weight_ref[0]).astype(BF16)
+
+    @pl.when(pl.program_id(0) == 0)
+    def _():
+        block = attn_ref.shape[1]
+        attn_ref[:, :, :features] = got_ref[:, slots : slots + block]
+        attn_ref[:, :, features:] = got_ref[:, slots + block :]
 
 
 def forward(sort, got, weight):
     adapters, features, hidden = weight.shape
     rows, received = sort.shape
     capacity = rows // adapters
+    slots = received // got.shape[0]
+    attn = (got.shape[0], (got.shape[1] - slots) // 2, 2 * features)
     return pl.pallas_call(
         forward_kernel,
         grid=(adapters,),
         out_shape=(
             jax.ShapeDtypeStruct((rows, features), BF16),
             jax.ShapeDtypeStruct((rows, hidden), BF16),
+            jax.ShapeDtypeStruct(attn, BF16),
         ),
         in_specs=[
             pl.BlockSpec((capacity, received), lambda a: (a, 0)),
-            pl.BlockSpec((received, features), lambda a: (0, 0)),
+            pl.BlockSpec(got.shape, lambda a: (0, 0, 0)),
             pl.BlockSpec((1, features, hidden), lambda a: (a, 0, 0)),
         ],
         out_specs=(
             pl.BlockSpec((capacity, features), lambda a: (a, 0)),
             pl.BlockSpec((capacity, hidden), lambda a: (a, 0)),
-        ),
-        compiler_params=pltpu.CompilerParams(vmem_limit_bytes=32 * 2**20),
+            pl.BlockSpec(attn, lambda a: (0, 0, 0)),
+        ),
+        compiler_params=pltpu.CompilerParams(vmem_limit_bytes=58 * 2**20),
         cost_estimate=pl.CostEstimate(flops=10**9, bytes_accessed=6 * 2**20, transcendentals=0),
     )(sort, got, weight)
 
@@ -193,10 +206,39 @@
             pl.BlockSpec((16, received), lambda a: (0, 0)),
         ),
         scratch_shapes=[pltpu.VMEM((rows, features + 128), BF16)],
-        compiler_params=pltpu.CompilerParams(vmem_limit_bytes=32 * 2**20),
+        compiler_params=pltpu.CompilerParams(vmem_limit_bytes=58 * 2**20),
         cost_estimate=pl.CostEstimate(flops=10**9, bytes_accessed=8 * 2**20, transcendentals=2**19),
     )(pre, bias[:, None], read_out[:, None], cot, weight, unsort)
     return half, bias_grad[:, 0], out_grad[:, 0], back, reward
+
+
+def pick_kernel(pick_ref, group_ref, attn_ref, out_ref):
+    owners, height, features = out_ref.shape
+    block = attn_ref.shape[0]
+    slots = height - 2 * block
+    chosen = pick_ref[0] + pick_ref[1]
+    out = mm(chosen, group_ref[...]).astype(BF16)
+    out_ref[:, :slots] = out.reshape(owners, slots, features)
+    for o in range(owners):
+        start = 2 * o * features
+        left = attn_ref[:, start : start + features]
+        right = attn_ref[:, start + features : start + 2 * features]
+        out_ref[o, slots:] = jnp.concatenate([left, right], axis=0)
+
+
+def call(kernel, outs, mflops, mbytes, *args):
+    vmem = pl.BlockSpec(memory_space=pltpu.VMEM)
+    smem = pl.BlockSpec(memory_space=pltpu.SMEM)
+    return pl.pallas_call(
+        kernel,
+        out_shape=tuple(jax.ShapeDtypeStruct(shape, dtype) for shape, dtype in outs),
+        in_specs=[smem if arg.ndim == 1 else vmem for arg in args],
+        out_specs=tuple(vmem for _ in outs),
+        compiler_params=pltpu.CompilerParams(vmem_limit_bytes=12 * 2**20),
+        cost_estimate=pl.CostEstimate(
+            flops=mflops * 10**6, bytes_accessed=mbytes * 2**20, transcendentals=0
+        ),
+    )(*args)
 
 
 def local(
@@ -212,10 +254,6 @@
     slots = 2 * rule_size
 
     group_rows = lax.all_to_all(hidden_states, "rule", split_axis=1, concat_axis=0, tiled=True)
-    attn_cols = lax.all_to_all(attn_input, "dp", split_axis=1, concat_axis=0, tiled=True)
-    attn_all = lax.all_gather(
-        attn_cols.reshape(dp_size, block, -1), "rule", axis=1, tiled=True
-    ).reshape(dp_size * tokens, -1)
 
     rule_all = rule_ids.T.reshape(2, dp_size, tokens)
     slot_all = slot_ids.T.reshape(2, dp_size, tokens)
@@ -224,11 +262,14 @@
     pos = jnp.where(slot_all >= 0, rule_all % adapters * capacity + slot_all, -1)
     me = lax.axis_index("dp").astype(jnp.int32).reshape(1)
     sort, unsort, pick, cot_rows = tables(block, rows, me, owner, pos, cot_all)
-    pick_sum = pick[0] + pick[1]
-
-    outgoing = mm(pick_sum, group_rows).astype(BF16)
+    (outgoing,) = call(
+        pick_kernel, [((dp_size, slots + 2 * block, feature_cols), BF16)], 200, 2,
+        pick, group_rows, attn_input,
+    )
     got = lax.all_to_all(outgoing, "dp", split_axis=0, concat_axis=0, tiled=True)
-    rows_buf, partial_pre = forward(sort, got, adapter_in)
+    rows_buf, partial_pre, attn_cols = forward(sort, got, adapter_in)
+    attn_all = lax.all_gather(attn_cols, "rule", axis=1, tiled=True)
+    attn_all = attn_all.reshape(dp_size * tokens, -1)
     shares = lax.all_to_all(partial_pre, "rule", split_axis=0, concat_axis=0, tiled=True)
     share = jnp.sum(
         shares.reshape(rule_size, rows // rule_size, hidden_units).astype(F32), axis=0
@@ -240,7 +281,8 @@
         preact, adapter_bias, adapter_out, cot_rows, adapter_in, unsort
     )
     returned = lax.all_to_all(back, "dp", split_axis=0, concat_axis=0, tiled=True)
-    state_grad = mm(pick_sum, returned, TN).astype(BF16)
+    state_grad = mm(pick[0] + pick[1], returned, TN).astype(BF16)
+    attn_all, state_grad = lax.optimization_barrier((attn_all, state_grad))
     state_all = lax.all_gather(state_grad, "dp", axis=0, tiled=True)
 
     reward_back = lax.all_to_all(

time: 235 us -> 228 us (0.970)
  blocking collectives: 109 us -> 94.3 us
  Pallas kernels: 11.5 us -> 21.9 us
  local copies, waits for them, and re-layouts: 13.3 us -> 10.3 us
  waiting for transfers between devices: 55.4 us -> 52.8 us
    all_to_all x1 -> x0, blocking collectives: 20.1 us -> none  [local(): lax.all_to_all(attn_input, 'dp', split_axis=1, concat_axis=0, tiled=True)]
    all_to_all x1, blocking collectives: 21.3 us -> 28.9 us  [local(): lax.all_to_all(outgoing, 'dp', split_axis=0, concat_axis=0, tiled=True)]
    pallas_call x1, Pallas kernels: 3.7 us -> 9.39 us  [backward(): pl.pallas_call(backward_kernel, grid=(adapters,), out_shape=(jax.ShapeDty...]
    unnamed x34 -> x24, local copies, waits for them, and re-layouts: 10.8 us -> 5.85 us
    pallas_call x1, Pallas kernels: 3.38 us -> 7.73 us  [forward(): pl.pallas_call(forward_kernel, grid=(adapters,), out_shape=(jax.ShapeDtyp...]
    all_to_all x1, starting transfers between devices: 10.7 us -> 13.9 us  [local(): lax.all_to_all(hidden_states, 'rule', split_axis=1, concat_axis=0, tiled=...]
    all_to_all x1, waiting for transfers between devices: 28.5 us -> 25.5 us  [local(): lax.all_to_all(share, 'rule', split_axis=0, concat_axis=0, tiled=True)]
    all_to_all x1, blocking collectives: 41.1 us -> 38.5 us  [local(): lax.all_to_all(partial_pre, 'rule', split_axis=0, concat_axis=0, tiled=True)]
  transfers between devices with their start and end apart: 5 -> 5, of which waited for: 3 -> 3; matrix products, arithmetic and copies ran while one was open for 3% -> 4% of each run, Pallas kernels for 5% -> 6%
where the time goes in v2:
time: 228 us; the launch traced here: 227 us
  blocking collectives  94.3 us (41%)
  waiting for transfers between devices  52.8 us (23%)
  starting transfers between devices  24.5 us (11%)
  Pallas kernels  21.9 us (10%)
  between operations  14.2 us (6%)
  local copies, waits for them, and re-layouts  10.3 us (5%)
  matrix products  8.16 us (4%)
    all_to_all x1, blocking collectives, local(): lax.all_to_all(partial_pre, 'rule', split_axis=0, concat_axis=0, tiled=True)  38.5 us
    all_to_all x1, blocking collectives, local(): lax.all_to_all(outgoing, 'dp', split_axis=0, concat_axis=0, tiled=True)  28.9 us
    all_to_all x1, blocking collectives, local(): lax.all_to_all(back, 'dp', split_axis=0, concat_axis=0, tiled=True)  26.9 us
    all_to_all x1, waiting for transfers between devices, local(): lax.all_to_all(share, 'rule', split_axis=0, concat_axis=0, tiled=True)  25.5 us
    all_gather x1, waiting for transfers between devices, local(): state_all = lax.all_gather(state_grad, 'dp', axis=0, tiled=True)  23.5 us
    all_to_all x1, starting transfers between devices, local(): lax.all_to_all(hidden_states, 'rule', split_axis=1, concat_axis=0, tiled=...  13.9 us
    pallas_call x1, Pallas kernels, backward(): pl.pallas_call(backward_kernel, grid=(adapters,), out_shape=(jax.ShapeDty...  9.39 us
    pallas_call x1, Pallas kernels, forward(): pl.pallas_call(forward_kernel, grid=(adapters,), out_shape=(jax.ShapeDtyp...  7.73 us
  transfers between devices with their start and end apart: 5, of which 3 were waited for; matrix products, arithmetic and copies ran while one was open for 4% of the time, Pallas kernels for 6%

profile of v2, /device:TPU:1, one launch (start us, length us, event | category | flops | bytes accessed | tf_op | source)
XLA Modules:
  0.0 227.1 jit_solution(5255312508616043708)
XLA Ops:
  7.2 13.9 %all-to-all-start = ((bf16[8,32,256]{2,0,1:T(8,128)(2,1)}), bf16[8,32,256]{2,0,1:T(8,128)(2,1)S(1)}, u32[]{:S(2)}, u32[]{:S(2)}) async-start(bf16[8,32,256]{2,0,1:T(8,128)(2,1)} %bitcast.82), calls=%async_computation | async-start | bytes 262144 | tf_op jit(solution)/shard_map/all_to_all | solution.py:256
  21.1 0.7 copy.51
  21.8 0.8 fusion.6
  22.6 4.4 %shard_map.119 = (bf16[1024,1024]{1,0:T(8,128)(2,1)S(1)}, bf16[1024,1024]{1,0:T(8,128)(2,1)S(1)}, bf16[2,1024,256]{2,1,0:T(8,128)(2,1)S(1)}, f32[1024,128]{1,0:T(8,128)S(1)}) custom-call(s32[1]{0:T(128)} %bitcast.me_ref, s32[2,16,256]{2,1,0:T(8,128)S(1)} %get-tuple-element.34.owner_ref, s32[2,16,256]{2,1,0:T(8,128)S(1)} %get-tuple-element.33.pos_ref, ...), custom_call_target="tpu_custom_call" | custom-call | flops 1000000000 | bytes 6291456 | tf_op jit(solution)/shard_map/pallas_call | solution.py:88
  27.1 1.3 copy-done
  28.4 1.4 copy-done.1
  29.7 0.8 copy-done.2
  30.9 28.9 %all_to_all.63.got_ref = bf16[16,80,256]{2,1,0:T(8,128)(2,1)} all-to-all(bf16[16,80,256]{2,1,0:T(8,128)(2,1)S(1)} %shard_map.120), channel_id=1, replica_groups=mesh['dp'=16,'rule'=32] {'dp'}, dimensions={0} | all-to-all | bytes 1310720 | tf_op jit(solution)/shard_map/all_to_all | solution.py:269
  59.8 7.7 %shard_map.121 = (bf16[1024,256]{1,0:T(8,128)(2,1)}, bf16[1024,512]{1,0:T(8,128)(2,1)}, bf16[16,8,512]{2,1,0:T(8,128)(2,1)}) custom-call(bf16[1024,1024]{1,0:T(8,128)(2,1)} %copy-done, bf16[16,80,256]{2,1,0:T(8,128)(2,1)} %all_to_all.63.got_ref, bf16[8,256,512]{2,1,0:T(8,128)(2,1)} %weight_ref.3), custom_call_target="tpu_custom_call" | custom-call | flops 1000000000 | bytes 6291456 | tf_op jit(solution)/shard_map/pallas_call | solution.py:124
  67.6 38.5 %all_to_all.64 = bf16[32,32,512]{2,1,0:T(8,128)(2,1)S(1)} all-to-all(bf16[32,32,512]{2,1,0:T(8,128)(2,1)} %bitcast.78), channel_id=1, replica_groups=mesh['dp'=16,'rule'=32] {'rule'}, dimensions={0} | all-to-all | bytes 2097152 | tf_op jit(solution)/shard_map/all_to_all | solution.py:273
  106.2 1.1 broadcast_in_dim.14
  107.3 7.2 %all-to-all-start.3 = ((bf16[32,32,512]{2,1,0:T(8,128)(2,1)}), bf16[32,32,512]{2,1,0:T(8,128)(2,1)S(1)}, u32[]{:S(2)}, u32[]{:S(2)}) async-start(bf16[32,32,512]{2,1,0:T(8,128)(2,1)} %broadcast_in_dim.14), calls=%async_computation.3 | async-start | bytes 2097152 | tf_op jit(solution)/shard_map/all_to_all | solution.py:278
  115.8 25.5 %all-to-all-done.3 = bf16[32,32,512]{2,1,0:T(8,128)(2,1)S(1)} async-done(((bf16[32,32,512]{2,1,0:T(8,128)(2,1)}), bf16[32,32,512]{2,1,0:T(8,128)(2,1)S(1)}, u32[]{:S(2)}, u32[]{:S(2)}) %all-to-all-start.3) | async-done | bytes 1048608 | tf_op jit(solution)/shard_map/all_to_all | solution.py:278
  141.3 1.0 copy-done.4
  142.3 9.4 %shard_map.122 = (bf16[1024,512]{1,0:T(8,128)(2,1)}, f32[8,1,512]{2,1,0:T(1,128)}, f32[8,1,512]{2,1,0:T(1,128)}, bf16[1024,256]{1,0:T(8,128)(2,1)}, bf16[16,1024]{1,0:T(8,128)(2,1)}) custom-call(bf16[1024,512]{1,0:T(8,128)(2,1)} %bitcast.76, f32[8,1,512]{2,1,0:T(1,128)} %broadcast_in_dim.15.bias_ref, f32[8,1,512]{2,1,0:T(1,128)} %broadcast_in_dim.16.out_ref, ...), custom_call_target="tpu_custom_call" | custom-call | flops 1000000000 | bytes 8388608 | tf_op jit(solution)/shard_map/pallas_call | solution.py:183
  151.7 26.9 %all_to_all.65 = bf16[16,64,256]{2,1,0:T(8,128)(2,1)S(1)} all-to-all(bf16[16,64,256]{2,1,0:T(8,128)(2,1)} %bitcast.80), channel_id=1, replica_groups=mesh['dp'=16,'rule'=32] {'dp'}, dimensions={0} | all-to-all | bytes 1048576 | tf_op jit(solution)/shard_map/all_to_all | solution.py:283
  178.6 1.1 convolution_convert_fusion.2
  179.7 0.7 slice_reduce_fusion
  180.5 0.7 all_to_all.56
  181.1 3.4 %all-to-all-start.4 = ((bf16[16,1,64]{2,1,0:T(2,128)(2,1)}), bf16[16,1,64]{2,1,0:T(2,128)(2,1)S(1)}, u32[]{:S(2)}, u32[]{:S(2)}) async-start(bf16[16,1,64]{2,1,0:T(2,128)(2,1)} %all_to_all.56), calls=%async_computation.4 | async-start | bytes 16384 | tf_op jit(solution)/shard_map/all_to_all | solution.py:288
  184.5 2.1 convolution_convert_fusion
  187.2 3.8 %all-to-all-done.4 = bf16[16,1,64]{2,1,0:T(2,128)(2,1)S(1)} async-done(((bf16[16,1,64]{2,1,0:T(2,128)(2,1)}), bf16[16,1,64]{2,1,0:T(2,128)(2,1)S(1)}, u32[]{:S(2)}, u32[]{:S(2)}) %all-to-all-start.4) | async-done | bytes 2080 | tf_op jit(solution)/shard_map/all_to_all | solution.py:288
  191.9 23.5 %all-gather.5.cloned.1.call-done = bf16[4096,256]{1,0:T(8,128)(2,1)} async-done(((bf16[256,256]{1,0:T(8,128)(2,1)}), bf16[4096,256]{1,0:T(8,128)(2,1)}) %all-gather.5.cloned.1.call-update) | async-done | bytes 2097168 | tf_op jit(solution)/shard_map/all_gather | solution.py:286
  215.5 4.8 %convolution_convert_fusion.1 = bf16[256,512]{1,0:T(8,128)(2,1)} fusion(bf16[4096,256]{1,0:T(8,128)(2,1)} %all-gather.5.cloned.1.call-done, bf16[4096,512]{1,0:T(8,128)(2,1)} %bitcast.87), kind=kOutput, calls=%fused_computation.1 | convolution fusion | flops 1073872896 | bytes 6553600 | tf_op jit(solution)/shard_map/dot_general | solution.py:18
  (33 shorter events, 3.4 us)
Async XLA Ops:
  7.2 23.4 %copy-start.3 = (bf16[8,8192]{1,0:T(8,128)(2,1)S(1)}, bf16[8,8192]{1,0:T(8,128)(2,1)}, u32[]{:S(2)}) copy-start(bf16[8,8192]{1,0:T(8,128)(2,1)} %attn_ref.1) | copy-start | bytes 393220
  7.2 23.4 %all-to-all-start = ((bf16[8,32,256]{2,0,1:T(8,128)(2,1)}), bf16[8,32,256]{2,0,1:T(8,128)(2,1)S(1)}, u32[]{:S(2)}, u32[]{:S(2)}) async-start(bf16[8,32,256]{2,0,1:T(8,128)(2,1)} %bitcast.82), calls=%async_computation | async-start | bytes 262144 | tf_op jit(solution)/shard_map/all_to_all | solution.py:256
  21.0 158.6 %all-gather.3.cloned.1.call-start = ((), (), s32[]{:S(2)}) async-start(), calls=%async_computation.6 | async-start | bytes 4325376 | tf_op jit(solution)/shard_map/all_gather | solution.py:271
  27.1 1.3 copy-start
  28.4 1.4 copy-start.1
  29.7 0.8 copy-start.2
  106.1 8.5 %copy-start.7 = (f32[8,512]{1,0:T(8,128)S(1)}, f32[8,512]{1,0:T(8,128)}, u32[]{:S(2)}) copy-start(f32[8,512]{1,0:T(8,128)} %param.14) | copy-start | bytes 49156
  106.1 9.2 %copy-start.8 = (f32[8,512]{1,0:T(8,128)S(1)}, f32[8,512]{1,0:T(8,128)}, u32[]{:S(2)}) copy-start(f32[8,512]{1,0:T(8,128)} %param.15) | copy-start | bytes 49156
  107.3 34.0 %all-to-all-start.3 = ((bf16[32,32,512]{2,1,0:T(8,128)(2,1)}), bf16[32,32,512]{2,1,0:T(8,128)(2,1)S(1)}, u32[]{:S(2)}, u32[]{:S(2)}) async-start(bf16[32,32,512]{2,1,0:T(8,128)(2,1)} %broadcast_in_dim.14), calls=%async_computation.3 | async-start | bytes 2097152 | tf_op jit(solution)/shard_map/all_to_all | solution.py:278
  114.6 100.9 %all-gather.5.cloned.1.call-start = ((), (), s32[]{:S(2)}) async-start(), calls=%async_computation.7 | async-start | bytes 2228224 | tf_op jit(solution)/shard_map/all_gather | solution.py:286
  141.3 1.0 copy-start.4
  151.7 32.8 %copy-start.5 = (bf16[1024,512]{1,0:T(8,128)(2,1)S(1)}, bf16[1024,512]{1,0:T(8,128)(2,1)}, u32[]{:S(2)}) copy-start(bf16[1024,512]{1,0:T(8,128)(2,1)} %get-tuple-element.26) | copy-start | bytes 3145732
  151.7 32.8 %copy-start.6 = (bf16[1024,256]{1,0:T(8,128)(2,1)S(1)}, bf16[1024,256]{1,0:T(8,128)(2,1)}, u32[]{:S(2)}) copy-start(bf16[1024,256]{1,0:T(8,128)(2,1)} %get-tuple-element.25) | copy-start | bytes 1572868
  179.7 6.9 %copy-start.9 = (f32[8,1,512]{2,1,0:T(1,128)S(1)}, f32[8,1,512]{2,1,0:T(1,128)}, u32[]{:S(2)}) copy-start(f32[8,1,512]{2,1,0:T(1,128)} %get-tuple-element.27) | copy-start | bytes 49156
  179.7 6.9 %copy-start.10 = (f32[8,1,512]{2,1,0:T(1,128)S(1)}, f32[8,1,512]{2,1,0:T(1,128)}, u32[]{:S(2)}) copy-start(f32[8,1,512]{2,1,0:T(1,128)} %get-tuple-element.28) | copy-start | bytes 49156
  181.1 9.9 %all-to-all-start.4 = ((bf16[16,1,64]{2,1,0:T(2,128)(2,1)}), bf16[16,1,64]{2,1,0:T(2,128)(2,1)S(1)}, u32[]{:S(2)}, u32[]{:S(2)}) async-start(bf16[16,1,64]{2,1,0:T(2,128)(2,1)} %all_to_all.56), calls=%async_computation.4 | async-start | bytes 16384 | tf_op jit(solution)/shard_map/all_to_all | solution.py:288
Sparse Core Ops, SparseCore 0:
  67.7 100.4 all-gather.2
  179.8 35.5 all-gather.4

commit v3 on v2

--- a/solution.py
+++ b/solution.py
@@ -100,116 +100,143 @@
     )(me, owner, pos, cot)
 
 
-def forward_kernel(sort_ref, got_ref, weight_ref, rows_ref, part_ref, attn_ref):
+def started(pairs, sems):
+    copies = []
+    for n, (source, target) in enumerate(pairs):
+        copies.append(pltpu.make_async_copy(source, target, sems.at[n]))
+        copies[-1].start()
+    return copies
+
+
+def forward_kernel(
+    sort_hbm, got_ref, weight_hbm, rows_hbm, part_ref, attn_hbm,
+    sort, weight, rows, attn, sort_sems, weight_sems, rows_sems, attn_sem,
+):
     groups, height, features = got_ref.shape
-    slots = sort_ref.shape[1] // groups
+    adapters = weight.shape[0]
+    capacity = sort.shape[0] // adapters
+    slots = sort.shape[1] // groups
+    at = [pl.ds(a * capacity, capacity) for a in range(adapters)]
+    sort_in = started([(sort_hbm.at[i], sort.at[i]) for i in at], sort_sems)
+    weight_in = started([(weight_hbm.at[a], weight.at[a]) for a in range(adapters)], weight_sems)
+    block = attn.shape[1]
+    attn[:, :, :features] = got_ref[:, slots : slots + block]
+    attn[:, :, features:] = got_ref[:, slots + block :]
+    out = started([(attn, attn_hbm)], attn_sem)
     got = got_ref[:, :slots].reshape(groups * slots, features)
-    rows = mm(sort_ref[...], got).astype(BF16)
-    rows_ref[...] = rows
-    part_ref[...] = mm(rows, weight_ref[0]).astype(BF16)
-
-    @pl.when(pl.program_id(0) == 0)
-    def _():
-        block = attn_ref.shape[1]
-        attn_ref[:, :, :features] = got_ref[:, slots : slots + block]
-        attn_ref[:, :, features:] = got_ref[:, slots + block :]
+    for a in range(adapters):
+        sort_in[a].wait()
+        rows[at[a]] = mm(sort[at[a]], got).astype(BF16)
+        copy = pltpu.make_async_copy(rows.at[at[a]], rows_hbm.at[at[a]], rows_sems.at[a])
+        copy.start()
+        out.append(copy)
+        weight_in[a].wait()
+        part_ref[at[a]] = mm(rows[at[a]], weight[a]).astype(BF16)
+    for copy in out:
+        copy.wait()
+
+
+ANYWHERE = pl.BlockSpec(memory_space=pl.ANY)
+IN_VMEM = pl.BlockSpec(memory_space=pltpu.VMEM)
 
 
 def forward(sort, got, weight):
     adapters, features, hidden = weight.shape
     rows, received = sort.shape
-    capacity = rows // adapters
     slots = received // got.shape[0]
     attn = (got.shape[0], (got.shape[1] - slots) // 2, 2 * features)
     return pl.pallas_call(
         forward_kernel,
-        grid=(adapters,),
         out_shape=(
             jax.ShapeDtypeStruct((rows, features), BF16),
             jax.ShapeDtypeStruct((rows, hidden), BF16),
             jax.ShapeDtypeStruct(attn, BF16),
         ),
-        in_specs=[
-            pl.BlockSpec((capacity, received), lambda a: (a, 0)),
-            pl.BlockSpec(got.shape, lambda a: (0, 0, 0)),
-            pl.BlockSpec((1, features, hidden), lambda a: (a, 0, 0)),
+        in_specs=[ANYWHERE, IN_VMEM, ANYWHERE],
+        out_specs=(ANYWHERE, IN_VMEM, ANYWHERE),
+        scratch_shapes=[
+            pltpu.VMEM(sort.shape, BF16),
+            pltpu.VMEM(weight.shape, BF16),
+            pltpu.VMEM((rows, features), BF16),
+            pltpu.VMEM(attn, BF16),
+            pltpu.SemaphoreType.DMA((adapters,)),
+            pltpu.SemaphoreType.DMA((adapters,)),
+            pltpu.SemaphoreType.DMA((adapters,)),
+            pltpu.SemaphoreType.DMA((1,)),
         ],
-        out_specs=(
-            pl.BlockSpec((capacity, features), lambda a: (a, 0)),
-            pl.BlockSpec((capacity, hidden), lambda a: (a, 0)),
-            pl.BlockSpec(attn, lambda a: (0, 0, 0)),
-        ),
         compiler_params=pltpu.CompilerParams(vmem_limit_bytes=58 * 2**20),
         cost_estimate=pl.CostEstimate(flops=10**9, bytes_accessed=6 * 2**20, transcendentals=0),
     )(sort, got, weight)
 
 
 def backward_kernel(
-    pre_ref, bias_ref, out_ref, cot_ref, weight_ref, unsort_ref,
-    half_ref, bias_grad_ref, out_grad_ref, back_ref, reward_ref, grads,
+    pre_ref, bias_ref, out_ref, cot_hbm, weight_hbm, unsort_hbm,
+    half_hbm, bias_grad_ref, out_grad_ref, back_ref, reward_ref,
+    cot_rows, weight, unsort, halves, grads, cot_sems, weight_sems, unsort_sems, half_sems,
 ):
-    a = pl.program_id(0)
-    capacity, hidden = pre_ref.shape
-    features = weight_ref.shape[1]
-    read_out = out_ref[0]
-    pre = pre_ref[...].astype(F32) + bias_ref[0]
-    s = 1.0 / (1.0 + jnp.exp(-pre))
-    cot = jnp.concatenate([cot_ref[...]] * (hidden // 128), axis=1)
-    activated = pre * s
-    grad_pre = cot * read_out * s * (1.0 + pre * (1.0 - s))
-    half = grad_pre.astype(BF16)
-    half_ref[...] = half
-    bias_grad_ref[0] = jnp.sum(grad_pre, axis=0, keepdims=True)
-    out_grad_ref[0] = jnp.sum(cot * activated, axis=0, keepdims=True)
-    reward = jnp.sum(activated * read_out, axis=1, keepdims=True)
-    at = pl.ds(pl.multiple_of(a * capacity, capacity), capacity)
-    grads[at, :features] = mm(half, weight_ref[0], NT).astype(BF16)
-    grads[at, features:] = jnp.broadcast_to(reward, (capacity, 128)).astype(BF16)
-
-    @pl.when(a == pl.num_programs(0) - 1)
-    def _():
-        back = mm(unsort_ref[...], grads[...]).astype(BF16)
-        back_ref[...] = back[:, :features]
-        first = lax.broadcasted_iota(jnp.int32, (16, 128), 1) == 0
-        first = jnp.where(first, 1.0, 0.0).astype(BF16)
-        reward_ref[...] = mm(first, back[:, features:], NT).astype(BF16)
+    adapters, features, hidden = weight.shape
+    capacity = pre_ref.shape[0] // adapters
+    at = [pl.ds(a * capacity, capacity) for a in range(adapters)]
+    (cot_in,) = started([(cot_hbm, cot_rows)], cot_sems)
+    weight_in = started([(weight_hbm.at[a], weight.at[a]) for a in range(adapters)], weight_sems)
+    (unsort_in,) = started([(unsort_hbm, unsort)], unsort_sems)
+    out = []
+    cot_in.wait()
+    for a in range(adapters):
+        read_out = out_ref[a : a + 1]
+        pre = pre_ref[at[a]].astype(F32) + bias_ref[a : a + 1]
+        s = 1.0 / (1.0 + jnp.exp(-pre))
+        cot = jnp.concatenate([cot_rows[at[a]]] * (hidden // 128), axis=1)
+        activated = pre * s
+        grad_pre = cot * read_out * s * (1.0 + pre * (1.0 - s))
+        halves[at[a]] = grad_pre.astype(BF16)
+        copy = pltpu.make_async_copy(halves.at[at[a]], half_hbm.at[at[a]], half_sems.at[a])
+        copy.start()
+        out.append(copy)
+        bias_grad_ref[a : a + 1] = jnp.sum(grad_pre, axis=0, keepdims=True)
+        out_grad_ref[a : a + 1] = jnp.sum(cot * activated, axis=0, keepdims=True)
+        reward = jnp.sum(activated * read_out, axis=1, keepdims=True)
+        grads[at[a], features:] = jnp.broadcast_to(reward, (capacity, 128)).astype(BF16)
+        weight_in[a].wait()
+        grads[at[a], :features] = mm(halves[at[a]], weight[a], NT).astype(BF16)
+    unsort_in.wait()
+    back = mm(unsort[...], grads[...]).astype(BF16)
+    back_ref[...] = back[:, :features]
+    first = lax.broadcasted_iota(jnp.int32, (16, 128), 1) == 0
+    first = jnp.where(first, 1.0, 0.0).astype(BF16)
+    reward_ref[...] = mm(first, back[:, features:], NT).astype(BF16)
+    for copy in out:
+        copy.wait()
 
 
 def backward(pre, bias, read_out, cot, weight, unsort):
     adapters, features, hidden = weight.shape
     received, rows = unsort.shape
-    capacity = rows // adapters
-    line = pl.BlockSpec((1, 1, hidden), lambda a: (a, 0, 0))
-    half, bias_grad, out_grad, back, reward = pl.pallas_call(
+    return pl.pallas_call(
         backward_kernel,
-        grid=(adapters,),
         out_shape=(
             jax.ShapeDtypeStruct((rows, hidden), BF16),
-            jax.ShapeDtypeStruct((adapters, 1, hidden), F32),
-            jax.ShapeDtypeStruct((adapters, 1, hidden), F32),
+            jax.ShapeDtypeStruct((adapters, hidden), F32),
+            jax.ShapeDtypeStruct((adapters, hidden), F32),
             jax.ShapeDtypeStruct((received, features), BF16),
             jax.ShapeDtypeStruct((16, received), BF16),
         ),
-        in_specs=[
-            pl.BlockSpec((capacity, hidden), lambda a: (a, 0)),
-            line,
-            line,
-            pl.BlockSpec((capacity, 128), lambda a: (a, 0)),
-            pl.BlockSpec((1, features, hidden), lambda a: (a, 0, 0)),
-            pl.BlockSpec((received, rows), lambda a: (0, 0)),
+        in_specs=[IN_VMEM, IN_VMEM, IN_VMEM, ANYWHERE, ANYWHERE, ANYWHERE],
+        out_specs=(ANYWHERE, IN_VMEM, IN_VMEM, IN_VMEM, IN_VMEM),
+        scratch_shapes=[
+            pltpu.VMEM(cot.shape, F32),
+            pltpu.VMEM(weight.shape, BF16),
+            pltpu.VMEM(unsort.shape, BF16),
+            pltpu.VMEM((rows, hidden), BF16),
+            pltpu.VMEM((rows, features + 128), BF16),
+            pltpu.SemaphoreType.DMA((1,)),
+            pltpu.SemaphoreType.DMA((adapters,)),
+            pltpu.SemaphoreType.DMA((1,)),
+            pltpu.SemaphoreType.DMA((adapters,)),
         ],
-        out_specs=(
-            pl.BlockSpec((capacity, hidden), lambda a: (a, 0)),
-            line,
-            line,
-            pl.BlockSpec((received, features), lambda a: (0, 0)),
-            pl.BlockSpec((16, received), lambda a: (0, 0)),
-        ),
-        scratch_shapes=[pltpu.VMEM((rows, features + 128), BF16)],
         compiler_params=pltpu.CompilerParams(vmem_limit_bytes=58 * 2**20),
         cost_estimate=pl.CostEstimate(flops=10**9, bytes_accessed=8 * 2**20, transcendentals=2**19),
-    )(pre, bias[:, None], read_out[:, None], cot, weight, unsort)
-    return half, bias_grad[:, 0], out_grad[:, 0], back, reward
+    )(pre, bias, read_out, cot, weight, unsort)
 
 
 def pick_kernel(pick_ref, group_ref, attn_ref, out_ref):
@@ -269,7 +296,6 @@
     got = lax.all_to_all(outgoing, "dp", split_axis=0, concat_axis=0, tiled=True)
     rows_buf, partial_pre, attn_cols = forward(sort, got, adapter_in)
     attn_all = lax.all_gather(attn_cols, "rule", axis=1, tiled=True)
-    attn_all = attn_all.reshape(dp_size * tokens, -1)
     shares = lax.all_to_all(partial_pre, "rule", split_axis=0, concat_axis=0, tiled=True)
     share = jnp.sum(
         shares.reshape(rule_size, rows // rule_size, hidden_units).astype(F32), axis=0
@@ -283,7 +309,12 @@
     returned = lax.all_to_all(back, "dp", split_axis=0, concat_axis=0, tiled=True)
     state_grad = mm(pick[0] + pick[1], returned, TN).astype(BF16)
     attn_all, state_grad = lax.optimization_barrier((attn_all, state_grad))
-    state_all = lax.all_gather(state_grad, "dp", axis=0, tiled=True)
+    cut = tokens // 2 - 8
+    width = attn_all.shape[2]
+    attn_low = attn_all[:, :cut].reshape(dp_size * cut, width)
+    attn_high = attn_all[:, cut:].reshape(dp_size * (tokens - cut), width)
+    state_low = lax.all_gather(state_grad[:cut], "dp", axis=0, tiled=True)
+    state_high = lax.all_gather(state_grad[cut:], "dp", axis=0, tiled=True)
 
     reward_back = lax.all_to_all(
         reward[0].reshape(dp_size, slots), "dp", split_axis=0, concat_axis=0, tiled=True
@@ -298,7 +329,8 @@
         grad_half.reshape(adapters, capacity, hidden_units),
         preferred_element_type=F32,
     ).astype(BF16)
-    o_proj_grad = mm(state_all, attn_all, TN).astype(BF16)
+    o_proj_grad = mm(state_low, attn_low, TN) + mm(state_high, attn_high, TN)
+    o_proj_grad = o_proj_grad.astype(BF16)
     return (rewards, in_grad, bias_grad, out_grad, o_proj_grad)
 
 

time: 228 us -> 222 us (0.974)
  blocking collectives: 94.3 us -> 147 us
  waiting for transfers between devices: 52.8 us -> 5.5 us
  starting transfers between devices: 24.5 us -> 17.3 us
    all_to_all x0 -> x1, blocking collectives: none -> 33.6 us  [local(): lax.all_to_all(share, 'rule', split_axis=0, concat_axis=0, tiled=True)]
    all_to_all x1 -> x0, waiting for transfers between devices: 25.5 us -> none  [local(): lax.all_to_all(share, 'rule', split_axis=0, concat_axis=0, tiled=True)]
    all_gather x1, waiting for transfers between devices: 23.5 us -> 0.84 us  [local(): state_high = lax.all_gather(state_grad[cut:], 'dp', axis=0, tiled=True)]
    all_gather x0 -> x1, blocking collectives: none -> 18.4 us  [local(): state_low = lax.all_gather(state_grad[:cut], 'dp', axis=0, tiled=True)]
    all_to_all x1 -> x0, starting transfers between devices: 7.21 us -> none  [local(): lax.all_to_all(share, 'rule', split_axis=0, concat_axis=0, tiled=True)]
    dot_general x2 -> x3, matrix products: 5.85 us -> 3.89 us  [mm(): return lax.dot_general(a, b, dims, preferred_element_type=F32)]
    unnamed x24 -> x17, local copies, waits for them, and re-layouts: 5.85 us -> 5.62 us
  transfers between devices with their start and end apart: 5 -> 4, of which waited for: 3 -> 2; matrix products, arithmetic and copies ran while one was open for 4% -> 3% of each run, Pallas kernels for 6% -> 6%
where the time goes in v3:
time: 222 us; the launch traced here: 221 us
  blocking collectives  147 us (66%)
  Pallas kernels  20.8 us (9%)
  starting transfers between devices  17.3 us (8%)
  between operations  14.2 us (6%)
  local copies, waits for them, and re-layouts  9.29 us (4%)
  matrix products  6.19 us (3%)
  waiting for transfers between devices  5.5 us (2%)
    all_to_all x1, blocking collectives, local(): lax.all_to_all(partial_pre, 'rule', split_axis=0, concat_axis=0, tiled=True)  38.5 us
    all_to_all x1, blocking collectives, local(): lax.all_to_all(share, 'rule', split_axis=0, concat_axis=0, tiled=True)  33.6 us
    all_to_all x1, blocking collectives, local(): lax.all_to_all(outgoing, 'dp', split_axis=0, concat_axis=0, tiled=True)  28.9 us
    all_to_all x1, blocking collectives, local(): lax.all_to_all(back, 'dp', split_axis=0, concat_axis=0, tiled=True)  27.1 us
    all_gather x1, blocking collectives, local(): state_low = lax.all_gather(state_grad[:cut], 'dp', axis=0, tiled=True)  18.4 us
    all_to_all x1, starting transfers between devices, local(): lax.all_to_all(hidden_states, 'rule', split_axis=1, concat_axis=0, tiled=...  13.9 us
    pallas_call x1, Pallas kernels, backward(): pl.pallas_call(backward_kernel, out_shape=(jax.ShapeDtypeStruct((rows, hi...  8.34 us
    pallas_call x1, Pallas kernels, forward(): pl.pallas_call(forward_kernel, out_shape=(jax.ShapeDtypeStruct((rows, fea...  7.73 us
  transfers between devices with their start and end apart: 4, of which 2 were waited for; matrix products, arithmetic and copies ran while one was open for 3% of the time, Pallas kernels for 6%

profile of v3, /device:TPU:1, one launch (start us, length us, event | category | flops | bytes accessed | tf_op | source)
XLA Modules:
  0.0 220.8 jit_solution(16251497156912870433)
XLA Ops:
  7.2 13.9 %all-to-all-start = ((bf16[8,32,256]{2,0,1:T(8,128)(2,1)}), bf16[8,32,256]{2,0,1:T(8,128)(2,1)S(1)}, u32[]{:S(2)}, u32[]{:S(2)}) async-start(bf16[8,32,256]{2,0,1:T(8,128)(2,1)} %bitcast.83), calls=%async_computation | async-start | bytes 262144 | tf_op jit(solution)/shard_map/all_to_all | solution.py:283
  21.1 0.7 copy.47
  21.8 0.8 fusion.7
  22.6 4.4 %shard_map.119 = (bf16[1024,1024]{1,0:T(8,128)(2,1)S(1)}, bf16[1024,1024]{1,0:T(8,128)(2,1)S(1)}, bf16[2,1024,256]{2,1,0:T(8,128)(2,1)S(1)}, f32[1024,128]{1,0:T(8,128)S(1)}) custom-call(s32[1]{0:T(128)} %bitcast.me_ref, s32[2,16,256]{2,1,0:T(8,128)S(1)} %get-tuple-element.34.owner_ref, s32[2,16,256]{2,1,0:T(8,128)S(1)} %get-tuple-element.33.pos_ref, ...), custom_call_target="tpu_custom_call" | custom-call | flops 1000000000 | bytes 6291456 | tf_op jit(solution)/shard_map/pallas_call | solution.py:88
  27.1 1.3 copy-done
  28.4 1.3 copy-done.1
  29.7 0.8 copy-done.2
  30.9 28.9 %all_to_all.63.got_ref = bf16[16,80,256]{2,1,0:T(8,128)(2,1)} all-to-all(bf16[16,80,256]{2,1,0:T(8,128)(2,1)S(1)} %shard_map.120), channel_id=1, replica_groups=mesh['dp'=16,'rule'=32] {'dp'}, dimensions={0} | all-to-all | bytes 1310720 | tf_op jit(solution)/shard_map/all_to_all | solution.py:296
  59.8 7.7 %shard_map.121 = (bf16[1024,256]{1,0:T(8,128)(2,1)}, bf16[1024,512]{1,0:T(8,128)(2,1)}, bf16[16,8,512]{2,1,0:T(8,128)(2,1)}) custom-call(bf16[1024,1024]{1,0:T(8,128)(2,1)} %copy-done, bf16[16,80,256]{2,1,0:T(8,128)(2,1)} %all_to_all.63.got_ref, bf16[8,256,512]{2,1,0:T(8,128)(2,1)} %weight_hbm.3), custom_call_target="tpu_custom_call" | custom-call | flops 1000000000 | bytes 6291456 | tf_op jit(solution)/shard_map/pallas_call | solution.py:148
  67.6 38.5 %all_to_all.64 = bf16[32,32,512]{2,1,0:T(8,128)(2,1)S(1)} all-to-all(bf16[32,32,512]{2,1,0:T(8,128)(2,1)} %bitcast.79), channel_id=1, replica_groups=mesh['dp'=16,'rule'=32] {'rule'}, dimensions={0} | all-to-all | bytes 2097152 | tf_op jit(solution)/shard_map/all_to_all | solution.py:299
  106.4 33.6 %all_to_all.65 = bf16[32,32,512]{2,1,0:T(8,128)(2,1)} all-to-all(bf16[32,32,512]{2,1,0:T(8,128)(2,1)S(1)} %broadcast_in_dim.4), channel_id=1, replica_groups=mesh['dp'=16,'rule'=32] {'rule'}, dimensions={0} | all-to-all | bytes 2097152 | tf_op jit(solution)/shard_map/all_to_all | solution.py:304
  140.0 8.3 %shard_map.122 = (bf16[1024,512]{1,0:T(8,128)(2,1)}, f32[8,512]{1,0:T(8,128)}, f32[8,512]{1,0:T(8,128)}, bf16[1024,256]{1,0:T(8,128)(2,1)}, bf16[16,1024]{1,0:T(8,128)(2,1)}) custom-call(bf16[1024,512]{1,0:T(8,128)(2,1)} %bitcast.76, f32[8,512]{1,0:T(8,128)} %bias_ref.1, f32[8,512]{1,0:T(8,128)} %out_ref.1, f32[1024,128]{1,0:T(8,128)} %copy-done.2, ...), custom_call_target="tpu_custom_call" | custom-call | flops 1000000000 | bytes 8388608 | tf_op jit(solution)/shard_map/pallas_call | solution.py:215
  148.3 27.1 %all_to_all.66 = bf16[16,64,256]{2,1,0:T(8,128)(2,1)S(1)} all-to-all(bf16[16,64,256]{2,1,0:T(8,128)(2,1)} %bitcast.81), channel_id=1, replica_groups=mesh['dp'=16,'rule'=32] {'dp'}, dimensions={0} | all-to-all | bytes 1048576 | tf_op jit(solution)/shard_map/all_to_all | solution.py:309
  176.6 0.7 slice_reduce_fusion
  177.3 0.7 all_to_all.56
  178.0 3.3 %all-to-all-start.4 = ((bf16[16,1,64]{2,1,0:T(2,128)(2,1)}), bf16[16,1,64]{2,1,0:T(2,128)(2,1)S(1)}, u32[]{:S(2)}, u32[]{:S(2)}) async-start(bf16[16,1,64]{2,1,0:T(2,128)(2,1)} %all_to_all.56), calls=%async_computation.4 | async-start | bytes 16384 | tf_op jit(solution)/shard_map/all_to_all | solution.py:319
  181.4 2.1 convolution_convert_fusion
  183.4 4.6 %all-to-all-done.4 = bf16[16,1,64]{2,1,0:T(2,128)(2,1)S(1)} async-done(((bf16[16,1,64]{2,1,0:T(2,128)(2,1)}), bf16[16,1,64]{2,1,0:T(2,128)(2,1)S(1)}, u32[]{:S(2)}, u32[]{:S(2)}) %all-to-all-start.4) | async-done | bytes 2080 | tf_op jit(solution)/shard_map/all_to_all | solution.py:319
  189.0 1.4 copy-done.4
  190.5 0.7 slice-done.1
  191.2 18.4 %all_gather.10 = bf16[1920,256]{1,0:T(8,128)(2,1)S(1)} all-gather(bf16[120,256]{1,0:T(8,128)(2,1)S(1)} %slice-done.1), channel_id=1, replica_groups=mesh['dp'=16,'rule'=32] {'dp'}, dimensions={0}, use_global_device_ids=true | all-gather | bytes 1044480 | tf_op jit(solution)/shard_map/all_gather | solution.py:316
  209.6 0.7 fusion.13
  210.3 0.8 all-gather.5.cloned.1.call-done
  211.2 2.7 %fusion = bf16[256,512]{1,0:T(8,128)(2,1)} fusion(f32[256,512]{1,0:T(8,128)S(1)} %fusion.13, bf16[2176,256]{1,0:T(8,128)(2,1)} %all-gather.5.cloned.1.call-done, bf16[2176,512]{1,0:T(8,128)(2,1)S(1)} %bitcast.77), kind=kOutput, calls=%fused_computation.2 | convolution fusion | flops 570687488 | bytes 4128768 | tf_op jit(solution)/shard_map/dot_general | solution.py:18
  (31 shorter events, 2.9 us)
Async XLA Ops:
  7.2 23.4 %copy-start.3 = (bf16[8,8192]{1,0:T(8,128)(2,1)S(1)}, bf16[8,8192]{1,0:T(8,128)(2,1)}, u32[]{:S(2)}) copy-start(bf16[8,8192]{1,0:T(8,128)(2,1)} %attn_ref.1) | copy-start | bytes 393220
  7.2 23.4 %all-to-all-start = ((bf16[8,32,256]{2,0,1:T(8,128)(2,1)}), bf16[8,32,256]{2,0,1:T(8,128)(2,1)S(1)}, u32[]{:S(2)}, u32[]{:S(2)}) async-start(bf16[8,32,256]{2,0,1:T(8,128)(2,1)} %bitcast.83), calls=%async_computation | async-start | bytes 262144 | tf_op jit(solution)/shard_map/all_to_all | solution.py:283
  21.0 154.9 %all-gather.3.cloned.1.call-start = ((), (), s32[]{:S(2)}) async-start(), calls=%async_computation.6 | async-start | bytes 4325376 | tf_op jit(solution)/shard_map/all_gather | solution.py:298
  27.1 1.3 copy-start
  28.4 1.4 copy-start.1
  29.7 0.8 copy-start.2
  67.6 143.6 %all-gather.5.cloned.1.call-start = ((), (), s32[]{:S(2)}) async-start(), calls=%async_computation.7 | async-start | bytes 1183744 | tf_op jit(solution)/shard_map/all_gather | solution.py:317
  148.3 33.1 %copy-start.5 = (bf16[1024,512]{1,0:T(8,128)(2,1)S(1)}, bf16[1024,512]{1,0:T(8,128)(2,1)}, u32[]{:S(2)}) copy-start(bf16[1024,512]{1,0:T(8,128)(2,1)} %get-tuple-element.26) | copy-start | bytes 3145732
  148.3 33.0 %copy-start.6 = (bf16[1024,256]{1,0:T(8,128)(2,1)S(1)}, bf16[1024,256]{1,0:T(8,128)(2,1)}, u32[]{:S(2)}) copy-start(bf16[1024,256]{1,0:T(8,128)(2,1)} %get-tuple-element.25) | copy-start | bytes 1572868
  175.9 13.1 %copy-start.7 = (bf16[256,256]{1,0:T(8,128)(2,1)}, bf16[256,256]{1,0:T(8,128)(2,1)S(1)}, u32[]{:S(2)}) copy-start(bf16[256,256]{1,0:T(8,128)(2,1)S(1)} %convolution_convert_fusion.1) | copy-start | bytes 393220
  178.0 10.0 %all-to-all-start.4 = ((bf16[16,1,64]{2,1,0:T(2,128)(2,1)}), bf16[16,1,64]{2,1,0:T(2,128)(2,1)S(1)}, u32[]{:S(2)}, u32[]{:S(2)}) async-start(bf16[16,1,64]{2,1,0:T(2,128)(2,1)} %all_to_all.56), calls=%async_computation.4 | async-start | bytes 16384 | tf_op jit(solution)/shard_map/all_to_all | solution.py:319
  188.2 2.2 copy-start.4
  190.4 0.8 slice-start.1
  190.4 19.3 %slice-start = ((bf16[16,256,512]{2,1,0:T(8,128)(2,1)}), bf16[16,120,512]{2,1,0:T(8,128)(2,1)S(1)}, s32[]{:S(2)}) async-start(bf16[16,256,512]{2,1,0:T(8,128)(2,1)} %all-gather.3.cloned.1.call-done), calls=%async_computation.8 | async-start | bytes 3932160 | tf_op jit(solution)/shard_map/slice | solution.py:314
Sparse Core Ops, SparseCore 0:
  67.7 99.0 all-gather.2
  176.7 34.4 all-gather.4

commit v4 on v3

v4 whole, which is shorter than its diff:
```python
import functools

import jax
import jax.numpy as jnp
from jax import lax
from jax.experimental import pallas as pl
from jax.experimental.pallas import tpu as pltpu
from jax.sharding import PartitionSpec as P

BF16 = jnp.bfloat16
F32 = jnp.float32
NN = (((1,), (0,)), ((), ()))
NT = (((1,), (1,)), ((), ()))
TN = (((0,), (0,)), ((), ()))


def mm(a, b, dims=NN):
    return lax.dot_general(a, b, dims, preferred_element_type=F32)


def select_kernel(adapters, rule_ref, slot_ref, hidden_ref, attn_ref, rows_ref, attn_out_ref):
    slices, owners, width = rows_ref.shape
    features = width // 2
    block = hidden_ref.shape[0]
    pairs = [(t, k) for t in range(block) for k in range(2)]
    owner = [rule_ref[k, t] // adapters for t, k in pairs]
    row = lax.broadcasted_iota(jnp.int32, (2 * owners, block), 0)
    token = lax.broadcasted_iota(jnp.int32, (2 * owners, block), 1)
    chosen = jnp.zeros((2 * owners, block), F32)
    for n, (t, k) in enumerate(pairs):
        rank = jnp.int32(0)
        for m in range(n):
            rank = rank + jnp.where(owner[m] == owner[n], 1, 0)
        key = jnp.where(slot_ref[k, t] >= 0, rank * owners + owner[n], -1)
        chosen = chosen + jnp.where((row == key) & (token == t), 1.0, 0.0)
    chosen = chosen.astype(BF16)
    for f in range(slices):
        out = mm(chosen, hidden_ref[:, f * features : (f + 1) * features]).astype(BF16)
        rows_ref[f, :, :features] = out[:owners]
        rows_ref[f, :, features:] = out[owners:]
    piece = attn_out_ref.shape[2]
    parts = slices // block
    for o in range(owners):
        for c in range(parts):
            start = (o * parts + c) * piece
            attn_out_ref[o, c * block : (c + 1) * block] = attn_ref[:, start : start + piece]


def tables_kernel(
    block, me_ref, owner_ref, pos_ref, cot_ref, lane_ref, row_ref, pick_ref, moved_ref, cot_out_ref
):
    me = me_ref[0]
    groups, tokens = owner_ref.shape[1:]
    rows = cot_out_ref.shape[0]
    blocks = tokens // block
    slots = 2 * blocks
    owner = [owner_ref[k] for k in range(2)]
    pos = [pos_ref[k] for k in range(2)]
    token = lax.broadcasted_iota(jnp.int32, (groups, tokens), 1)
    in_block = token % block
    rank = [jnp.zeros((groups, tokens), jnp.int32), (owner[0] == owner[1]).astype(jnp.int32)]
    for shift in range(1, block):
        for other in range(2):
            moved = pltpu.roll(owner[other], shift, 1)
            for k in range(2):
                hit = (moved == owner[k]) & (in_block >= shift)
                rank[k] = rank[k] + hit.astype(jnp.int32)
    place = [rank[k] * blocks + token // block for k in range(2)]
    held = [pos[k] >= 0 for k in range(2)]

    mine = lax.broadcasted_iota(jnp.int32, (groups, tokens), 0) == me
    slot_row = lax.broadcasted_iota(jnp.int32, (groups * slots, tokens), 0)
    total = jnp.zeros((groups * slots, tokens), F32)
    for k in range(2):
        key = jnp.where(held[k], owner[k] * slots + place[k], -1)
        key = jnp.sum(jnp.where(mine, key, 0), axis=0, keepdims=True)
        pick = jnp.where(slot_row == key, 1.0, 0.0)
        total = total + pick
        pick_ref[k] = pick.astype(BF16)
    before = lax.broadcasted_iota(jnp.int32, (tokens, tokens), 0)
    after = lax.broadcasted_iota(jnp.int32, (tokens, tokens), 1)
    order = jnp.where(before % block * blocks + before // block == after, 1.0, 0.0).astype(BF16)
    moved_ref[...] = mm(total.astype(BF16), order).astype(BF16)

    received = [jnp.where(held[k] & (owner[k] == me), place[k], -1) for k in range(2)]
    high = [((pos[k] + 1) // 32).astype(F32).astype(BF16) for k in range(2)]
    low = [((pos[k] + 1) % 32).astype(F32).astype(BF16) for k in range(2)]
    cot = [cot_ref[k] for k in range(2)]
    batch = 128 // blocks
    steps = groups // batch
    cot_total = jnp.zeros((rows, 128), F32)
    lane_row = lax.broadcasted_iota(jnp.int32, (128, tokens), 0)
    buffer_row = lax.broadcasted_iota(jnp.int32, (rows, 128), 0)
    for r in range(2):
        for step in range(steps):
            ones, highs, lows, cots = [], [], [], []
            for part in range(batch):
                g = step * batch + part
                for k in range(2):
                    row = received[k][g : g + 1] - r * blocks
                    row = jnp.where((row >= 0) & (row < blocks), row + part * blocks, -1)
                    ones.append(jnp.where(lane_row == row, 1.0, 0.0).astype(BF16))
                    highs.append(high[k][g : g + 1])
                    lows.append(low[k][g : g + 1])
                    cots.append(cot[k][g : g + 1])
            chosen = jnp.concatenate(ones, axis=1)
            wide = chosen.shape[1]
            high_row = jnp.broadcast_to(jnp.concatenate(highs, axis=1), (128, wide))
            low_row = jnp.broadcast_to(jnp.concatenate(lows, axis=1), (128, wide))
            cot_row = jnp.broadcast_to(jnp.concatenate(cots, axis=1), (128, wide))
            at_lane = mm(high_row, chosen, NT) * 32.0 + mm(low_row, chosen, NT)
            at_lane = at_lane.astype(jnp.int32) - 1
            at_row = mm(chosen, high_row, NT) * 32.0 + mm(chosen, low_row, NT)
            at_row = at_row.astype(jnp.int32) - 1
            cot_lane = mm(cot_row, chosen, NT).astype(BF16)
            hit = jnp.where(buffer_row == at_lane[0:1], 1.0, 0.0).astype(BF16)
            cot_total = cot_total + mm(hit, cot_lane, NT)
            lane = (r * steps + step) * 128
            lane_ref[:, lane : lane + 128] = at_lane[0:8]
            for part in range(batch):
                at = (step * batch + part) * slots + r * blocks
                row_ref[at : at + blocks] = at_row[part * blocks : (part + 1) * blocks]
    cot_out_ref[...] = cot_total


def started(pairs, sems):
    copies = []
    for n, (source, target) in enumerate(pairs):
        copies.append(pltpu.make_async_copy(source, target, sems.at[n]))
        copies[-1].start()
    return copies


def forward_kernel(
    lane_ref, got_ref, weight_hbm, rows_hbm, part_ref, attn_hbm,
    weight, rows, attn, weight_sems, rows_sem, attn_sem,
):
    adapters, features, hidden = weight.shape
    capacity = rows.shape[0] // adapters
    blocks = got_ref.shape[0]
    weight_in = started([(weight_hbm.at[a], weight.at[a]) for a in range(adapters)], weight_sems)
    attn[...] = got_ref[:, 2 * features :]
    (attn_out,) = started([(attn, attn_hbm)], attn_sem)
    buffer_row = lax.broadcasted_iota(jnp.int32, (rows.shape[0], blocks), 0)
    total = jnp.zeros(rows.shape, F32)
    for r in range(2):
        hit = buffer_row == lane_ref[0:1, r * blocks : (r + 1) * blocks]
        hit = jnp.where(hit, 1.0, 0.0).astype(BF16)
        total = total + mm(hit, got_ref[:, r * features : (r + 1) * features])
    rows[...] = total.astype(BF16)
    (rows_out,) = started([(rows, rows_hbm)], rows_sem)
    for a in range(adapters):
        weight_in[a].wait()
        at = slice(a * capacity, (a + 1) * capacity)
        part_ref[at] = mm(rows[at], weight[a]).astype(BF16)
    attn_out.wait()
    rows_out.wait()


ANYWHERE = pl.BlockSpec(memory_space=pl.ANY)
IN_VMEM = pl.BlockSpec(memory_space=pltpu.VMEM)


def forward(lane, got, weight):
    adapters, features, hidden = weight.shape
    rows = lane.shape[1]
    attn = (got.shape[0], got.shape[1] - 2 * features)
    return pl.pallas_call(
        forward_kernel,
        out_shape=(
            jax.ShapeDtypeStruct((rows, features), BF16),
            jax.ShapeDtypeStruct((rows, hidden), BF16),
            jax.ShapeDtypeStruct(attn, BF16),
        ),
        in_specs=[IN_VMEM, IN_VMEM, ANYWHERE],
        out_specs=(ANYWHERE, IN_VMEM, ANYWHERE),
        scratch_shapes=[
            pltpu.VMEM(weight.shape, BF16),
            pltpu.VMEM((rows, features), BF16),
            pltpu.VMEM(attn, BF16),
            pltpu.SemaphoreType.DMA((adapters,)),
            pltpu.SemaphoreType.DMA((1,)),
            pltpu.SemaphoreType.DMA((1,)),
        ],
        compiler_params=pltpu.CompilerParams(vmem_limit_bytes=56 * 2**20),
        cost_estimate=pl.CostEstimate(flops=10**9, bytes_accessed=6 * 2**20, transcendentals=0),
    )(lane, got, weight)


def backward_kernel(
    pre_ref, bias_ref, out_ref, cot_hbm, weight_hbm, row_hbm,
    half_hbm, bias_grad_ref, out_grad_ref, back_ref, reward_ref,
    cot_rows, weight, unsort, row, halves, grads, cot_sems, weight_sems, row_sems, half_sems,
):
    adapters, features, hidden = weight.shape
    capacity = pre_ref.shape[0] // adapters
    at = [pl.ds(a * capacity, capacity) for a in range(adapters)]
    (cot_in,) = started([(cot_hbm, cot_rows)], cot_sems)
    weight_in = started([(weight_hbm.at[a], weight.at[a]) for a in range(adapters)], weight_sems)
    (row_in,) = started([(row_hbm, row)], row_sems)
    out = []
    cot_in.wait()
    row_in.wait()
    lane = lax.broadcasted_iota(jnp.int32, (capacity, 128), 1)
    for a in range(adapters):
        for n in range(0, unsort.shape[1], 128):
            hit = row[at[a]] - n == lane
            unsort[at[a], n : n + 128] = jnp.where(hit, 1.0, 0.0).astype(BF16)
    for a in range(adapters):
        read_out = out_ref[a : a + 1]
        pre = pre_ref[at[a]].astype(F32) + bias_ref[a : a + 1]
        s = 1.0 / (1.0 + jnp.exp(-pre))
        cot = jnp.concatenate([cot_rows[at[a]]] * (hidden // 128), axis=1)
        activated = pre * s
        grad_pre = cot * read_out * s * (1.0 + pre * (1.0 - s))
        halves[at[a]] = grad_pre.astype(BF16)
        copy = pltpu.make_async_copy(halves.at[at[a]], half_hbm.at[at[a]], half_sems.at[a])
        copy.start()
        out.append(copy)
        bias_grad_ref[a : a + 1] = jnp.sum(grad_pre, axis=0, keepdims=True)
        out_grad_ref[a : a + 1] = jnp.sum(cot * activated, axis=0, keepdims=True)
        reward = jnp.sum(activated * read_out, axis=1, keepdims=True)
        grads[at[a], features:] = jnp.broadcast_to(reward, (capacity, 128)).astype(BF16)
        weight_in[a].wait()
        grads[at[a], :features] = mm(halves[at[a]], weight[a], NT).astype(BF16)
    back = mm(unsort[...], grads[...]).astype(BF16)
    back_ref[...] = back[:, :features]
    first = lax.broadcasted_iota(jnp.int32, (16, 128), 1) == 0
    first = jnp.where(first, 1.0, 0.0).astype(BF16)
    reward_ref[...] = mm(first, back[:, features:], NT).astype(BF16)
    for copy in out:
        copy.wait()


def backward(pre, bias, read_out, cot, weight, row):
    adapters, features, hidden = weight.shape
    received, rows = row.shape[0], pre.shape[0]
    return pl.pallas_call(
        backward_kernel,
        out_shape=(
            jax.ShapeDtypeStruct((rows, hidden), BF16),
            jax.ShapeDtypeStruct((adapters, hidden), F32),
            jax.ShapeDtypeStruct((adapters, hidden), F32),
            jax.ShapeDtypeStruct((received, features), BF16),
            jax.ShapeDtypeStruct((16, received), BF16),
        ),
        in_specs=[IN_VMEM, IN_VMEM, IN_VMEM, ANYWHERE, ANYWHERE, ANYWHERE],
        out_specs=(ANYWHERE, IN_VMEM, IN_VMEM, IN_VMEM, IN_VMEM),
        scratch_shapes=[
            pltpu.VMEM(cot.shape, F32),
            pltpu.VMEM(weight.shape, BF16),
            pltpu.VMEM((received, rows), BF16),
            pltpu.VMEM(row.shape, jnp.int32),
            pltpu.VMEM((rows, hidden), BF16),
            pltpu.VMEM((rows, features + 128), BF16),
            pltpu.SemaphoreType.DMA((1,)),
            pltpu.SemaphoreType.DMA((adapters,)),
            pltpu.SemaphoreType.DMA((1,)),
            pltpu.SemaphoreType.DMA((adapters,)),
        ],
        compiler_params=pltpu.CompilerParams(vmem_limit_bytes=58 * 2**20),
        cost_estimate=pl.CostEstimate(flops=10**9, bytes_accessed=8 * 2**20, transcendentals=2**19),
    )(pre, bias, read_out, cot, weight, row)


def project_kernel(state_hbm, attn_ref, out_ref, state, sems):
    block, groups, blocks, features = state.shape
    parts = attn_ref.shape[0]
    state_in = started([(state_hbm.at[:, t], state.at[t]) for t in range(block)], sems)
    total = jnp.zeros(out_ref.shape, F32)
    for t in range(block):
        columns = jnp.concatenate([attn_ref[c, t] for c in range(parts)], axis=1)
        state_in[t].wait()
        total = total + mm(state[t].reshape(groups * blocks, features), columns, TN)
    out_ref[...] = total.astype(BF16)


def project(state, attn):
    groups, block, blocks, features = state.shape
    return pl.pallas_call(
        project_kernel,
        out_shape=jax.ShapeDtypeStruct((features, attn.shape[0] * attn.shape[3]), BF16),
        in_specs=[ANYWHERE, IN_VMEM],
        out_specs=IN_VMEM,
        scratch_shapes=[
            pltpu.VMEM((block, groups, blocks, features), BF16),
            pltpu.SemaphoreType.DMA((block,)),
        ],
        compiler_params=pltpu.CompilerParams(vmem_limit_bytes=52 * 2**20),
        cost_estimate=pl.CostEstimate(flops=10**9, bytes_accessed=6 * 2**20, transcendentals=0),
    )(state, attn)


def local(
    hidden_states, attn_input, rule_ids, slot_ids, cotangent, adapter_in, adapter_bias, adapter_out
):
    dp_size = lax.axis_size("dp")
    rule_size = lax.axis_size("rule")
    block = hidden_states.shape[0]
    adapters, feature_cols, hidden_units = adapter_in.shape
    tokens = block * rule_size
    capacity = 4 * block * rule_size // adapters
    rows = adapters * capacity
    slots = 2 * rule_size

    me = lax.axis_index("dp").astype(jnp.int32)
    first = (me * rule_size + lax.axis_index("rule").astype(jnp.int32)) * block
    rules, slot = rule_ids.T, slot_ids.T
    piece = 2 * feature_cols * block // rule_size
    select_out = (
        jax.ShapeDtypeStruct((rule_size, dp_size, 2 * feature_cols), BF16),
        jax.ShapeDtypeStruct((dp_size, rule_size, piece), BF16),
    )
    in_smem = pl.BlockSpec(memory_space=pltpu.SMEM)
    rows_out, attn_out = pl.pallas_call(
        functools.partial(select_kernel, adapters),
        out_shape=select_out,
        in_specs=[in_smem, in_smem, IN_VMEM, IN_VMEM],
        out_specs=(IN_VMEM, IN_VMEM),
        compiler_params=pltpu.CompilerParams(vmem_limit_bytes=8 * 2**20),
        cost_estimate=pl.CostEstimate(flops=10**8, bytes_accessed=2**20, transcendentals=0),
    )(
        lax.dynamic_slice(rules, (0, first), (2, block)),
        lax.dynamic_slice(slot, (0, first), (2, block)),
        hidden_states,
        attn_input,
    )
    outgoing = jnp.concatenate([jnp.swapaxes(rows_out, 0, 1), attn_out], axis=2)
    outgoing = outgoing.reshape(dp_size * rule_size, 2 * feature_cols + piece)
    got = lax.all_to_all(outgoing, ("dp", "rule"), split_axis=0, concat_axis=0, tiled=True)

    rule_all = rules.reshape(2, dp_size, tokens)
    slot_all = slot.reshape(2, dp_size, tokens)
    cot_all = cotangent.T.reshape(2, dp_size, tokens)
    owner = rule_all // adapters
    pos = jnp.where(slot_all >= 0, rule_all % adapters * capacity + slot_all, -1)
    received = dp_size * slots
    lane, row, pick, pick_moved, cot_rows = pl.pallas_call(
        functools.partial(tables_kernel, block),
        out_shape=(
            jax.ShapeDtypeStruct((8, received), jnp.int32),
            jax.ShapeDtypeStruct((received, 128), jnp.int32),
            jax.ShapeDtypeStruct((2, received, tokens), BF16),
            jax.ShapeDtypeStruct((received, tokens), BF16),
            jax.ShapeDtypeStruct((rows, 128), F32),
        ),
        in_specs=[in_smem, IN_VMEM, IN_VMEM, IN_VMEM],
        out_specs=(IN_VMEM,) * 5,
        compiler_params=pltpu.CompilerParams(vmem_limit_bytes=24 * 2**20),
        cost_estimate=pl.CostEstimate(flops=10**9, bytes_accessed=2**22, transcendentals=0),
    )(me.reshape(1), owner, pos, cot_all)

    rows_buf, partial_pre, attn_cols = forward(lane, got, adapter_in)
    attn_all = lax.all_gather(attn_cols, "rule", axis=0, tiled=True)
    attn_all = attn_all.reshape(rule_size // block, block, dp_size * rule_size, piece)
    shares = lax.all_to_all(partial_pre, "rule", split_axis=0, concat_axis=0, tiled=True)
    share = jnp.sum(
        shares.reshape(rule_size, rows // rule_size, hidden_units).astype(F32), axis=0
    ).astype(BF16)
    share = jnp.broadcast_to(share[None], (rule_size,) + share.shape).reshape(rows, hidden_units)
    preact = lax.all_to_all(share, "rule", split_axis=0, concat_axis=0, tiled=True)

    grad_half, bias_grad, out_grad, back, reward = backward(
        preact, adapter_bias, adapter_out, cot_rows, adapter_in, row
    )
    returned = lax.all_to_all(back, "dp", split_axis=0, concat_axis=0, tiled=True)
    state_grad = mm(pick_moved, returned, TN).astype(BF16)
    attn_all, state_grad = lax.optimization_barrier((attn_all, state_grad))
    state_all = lax.all_gather(state_grad, "dp", axis=0, tiled=True)
    state_all = state_all.reshape(dp_size, block, rule_size, feature_cols)

    reward_back = lax.all_to_all(
        reward[0].reshape(dp_size, slots), "dp", split_axis=0, concat_axis=0, tiled=True
    )
    rewards = lax.dot_general(
        pick, reward_back.reshape(-1), (((1,), (0,)), ((), ())), preferred_element_type=F32
    )
    rewards = rewards.astype(BF16).T
    in_grad = jnp.einsum(
        "acd,acr->adr",
        rows_buf.reshape(adapters, capacity, feature_cols),
        grad_half.reshape(adapters, capacity, hidden_units),
        preferred_element_type=F32,
    ).astype(BF16)
    o_proj_grad = project(state_all, attn_all)
    return (rewards, in_grad, bias_grad, out_grad, o_proj_grad)


def solution(mesh):
    placed = (
        P(("dp", "rule"), None),
        P(("dp", "rule"), None),
        P(),
        P(),
        P(),
        P("dp", "rule", None),
        P("dp", None),
        P("dp", None),
    )
    return jax.shard_map(
        local,
        mesh=mesh,
        in_specs=placed,
        out_specs=(
            P("dp", None),
            P("dp", "rule", None),
            P("dp", None),
            P("dp", None),
            P("rule", "dp"),
        ),
        check_vma=False,
    )
```

time: 222 us -> 234 us (1.054)
  blocking collectives: 147 us -> 99.4 us
  waiting for transfers between devices: 5.5 us -> 45.1 us
  starting transfers between devices: 17.3 us -> 27.6 us
  Pallas kernels: 20.8 us -> 27.7 us
  local copies, waits for them, and re-layouts: 9.29 us -> 14.7 us
  matrix products: 6.19 us -> 3.3 us
    all_to_all x1 -> x0, blocking collectives: 28.9 us -> none  [local(): lax.all_to_all(outgoing, 'dp', split_axis=0, concat_axis=0, tiled=True)]
    all_gather x2, waiting for transfers between devices: 0.86 us -> 24.9 us  [the longest x1 24.9 us: local(): state_all = lax.all_gather(state_grad, 'dp', axis=0, tiled=True)]
    all_gather x1 -> x0, blocking collectives: 18.4 us -> none  [local(): state_low = lax.all_gather(state_grad[:cut], 'dp', axis=0, tiled=True)]
    all_to_all x1, waiting for transfers between devices: 0.01 us -> 15.9 us  [local(): lax.all_to_all(outgoing, ('dp', 'rule'), split_axis=0, concat_axis=0, til...]
    all_to_all x1, starting transfers between devices: 13.9 us -> 24 us  [local(): lax.all_to_all(outgoing, ('dp', 'rule'), split_axis=0, concat_axis=0, til...]
    pallas_call x2 -> x3, Pallas kernels: 4.72 us -> 13.8 us  [the longest x1 6.88 us: local(): pl.pallas_call(functools.partial(tables_kernel, block), out_shape=(jax.Sh...]
    unnamed x17 -> x24, local copies, waits for them, and re-layouts: 5.62 us -> 11.1 us
    all_to_all x1, blocking collectives: 38.5 us -> 34.4 us  [local(): lax.all_to_all(partial_pre, 'rule', split_axis=0, concat_axis=0, tiled=True)]
  transfers between devices with their start and end apart: 4 -> 4, of which waited for: 2 -> 3; matrix products, arithmetic and copies ran while one was open for 3% -> 2% of each run, Pallas kernels for 6% -> 7%
where the time goes in v4:
time: 234 us
  blocking collectives  99.4 us (42%)
  waiting for transfers between devices  45.1 us (19%)
  Pallas kernels  27.7 us (12%)
  starting transfers between devices  27.6 us (12%)
  local copies, waits for them, and re-layouts  14.7 us (6%)
  between operations  14.2 us (6%)
  matrix products  3.3 us (1%)
    all_to_all x1, blocking collectives, local(): lax.all_to_all(share, 'rule', split_axis=0, concat_axis=0, tiled=True)  37.5 us
    all_to_all x1, blocking collectives, local(): lax.all_to_all(partial_pre, 'rule', split_axis=0, concat_axis=0, tiled=True)  34.4 us
    all_to_all x1, blocking collectives, local(): lax.all_to_all(back, 'dp', split_axis=0, concat_axis=0, tiled=True)  27.5 us
    all_gather x1, waiting for transfers between devices, local(): state_all = lax.all_gather(state_grad, 'dp', axis=0, tiled=True)  24.9 us
    all_to_all x1, starting transfers between devices, local(): lax.all_to_all(outgoing, ('dp', 'rule'), split_axis=0, concat_axis=0, til...  24 us
    all_to_all x1, waiting for transfers between devices, local(): lax.all_to_all(outgoing, ('dp', 'rule'), split_axis=0, concat_axis=0, til...  15.9 us
    unnamed x24, local copies, waits for them, and re-layouts  11.1 us
    pallas_call x1, Pallas kernels, backward(): pl.pallas_call(backward_kernel, out_shape=(jax.ShapeDtypeStruct((rows, hi...  9 us
  transfers between devices with their start and end apart: 4, of which 3 were waited for; matrix products, arithmetic and copies ran while one was open for 2% of the time, Pallas kernels for 7%

profile of v4, /device:TPU:1, one launch (start us, length us, event | category | flops | bytes accessed | tf_op | source)
XLA Modules:
  0.0 233.6 jit_solution(3129257021834778151)
XLA Ops:
  7.2 0.8 dynamic-slice_bitcast_fusion
  7.9 0.9 copy-done.2
  8.9 0.9 copy-done.3
  9.8 1.0 shard_map.120
  11.6 1.1 reduce.5
  12.7 1.5 reshape.70
  14.2 24.0 %all-to-all-start = ((bf16[512,2,320]{2,1,0:T(2,128)(2,1)}), bf16[512,2,320]{2,1,0:T(2,128)(2,1)}, u32[]{:S(2)}, u32[]{:S(2)}) async-start(bf16[512,2,320]{2,1,0:T(2,128)(2,1)} %reshape.70), calls=%async_computation | async-start | bytes 1572864 | tf_op jit(solution)/shard_map/all_to_all | solution.py:330
  38.5 6.9 %shard_map.119 = (s32[8,1024]{1,0:T(8,128)S(1)}, s32[1024,128]{1,0:T(8,128)S(1)}, bf16[2,1024,256]{2,1,0:T(8,128)(2,1)S(1)}, bf16[1024,256]{1,0:T(8,128)(2,1)S(1)}, f32[1024,128]{1,0:T(8,128)S(1)}) custom-call(s32[1]{0:T(128)} %bitcast.me_ref, s32[2,16,256]{2,1,0:T(8,128)S(1)} %get-tuple-element.40.owner_ref, s32[2,16,256]{2,1,0:T(8,128)S(1)} %get-tuple-element.39.pos_ref, ...), custom_call_target="tpu_custom_call" | custom-call | flops 1000000000 | bytes 4194304 | tf_op jit(solution)/shard_map/pallas_call | solution.py:338
  45.4 0.8 copy-done
  46.2 0.8 copy-done.1
  47.7 15.9 %all-to-all-done = bf16[512,2,320]{2,1,0:T(2,128)(2,1)} async-done(((bf16[512,2,320]{2,1,0:T(2,128)(2,1)}), bf16[512,2,320]{2,1,0:T(2,128)(2,1)}, u32[]{:S(2)}, u32[]{:S(2)}) %all-to-all-start) | async-done | bytes 655392 | tf_op jit(solution)/shard_map/all_to_all | solution.py:330
  63.5 4.5 %reshape.71 = bf16[512,1,640]{2,1,0:T(2,128)(2,1)S(1)} reshape(bf16[512,2,320]{2,1,0:T(2,128)(2,1)} %all-to-all-done) | data formatting | bytes 1310720
  68.1 0.9 copy.55
  69.0 4.9 %shard_map.121 = (bf16[1024,256]{1,0:T(8,128)(2,1)}, bf16[1024,512]{1,0:T(8,128)(2,1)}, bf16[512,128]{1,0:T(8,128)(2,1)}) custom-call(s32[8,1024]{1,0:T(8,128)} %copy-done.4, bf16[512,640]{1,0:T(8,128)(2,1)} %bitcast.80, bf16[8,256,512]{2,1,0:T(8,128)(2,1)} %weight_hbm.3), custom_call_target="tpu_custom_call" | custom-call | flops 1000000000 | bytes 6291456 | tf_op jit(solution)/shard_map/pallas_call | solution.py:168
  74.0 34.4 %all_to_all.50 = bf16[32,32,512]{2,1,0:T(8,128)(2,1)S(1)} all-to-all(bf16[32,32,512]{2,1,0:T(8,128)(2,1)} %bitcast.79), channel_id=1, replica_groups=mesh['dp'=16,'rule'=32] {'rule'}, dimensions={0} | all-to-all | bytes 2097152 | tf_op jit(solution)/shard_map/all_to_all | solution.py:356
  108.7 37.5 %all_to_all.51 = bf16[32,32,512]{2,1,0:T(8,128)(2,1)} all-to-all(bf16[32,32,512]{2,1,0:T(8,128)(2,1)S(1)} %broadcast_in_dim.4), channel_id=1, replica_groups=mesh['dp'=16,'rule'=32] {'rule'}, dimensions={0} | all-to-all | bytes 2097152 | tf_op jit(solution)/shard_map/all_to_all | solution.py:361
  146.2 9.0 %shard_map.122 = (bf16[1024,512]{1,0:T(8,128)(2,1)}, f32[8,512]{1,0:T(8,128)}, f32[8,512]{1,0:T(8,128)}, bf16[1024,256]{1,0:T(8,128)(2,1)}, bf16[16,1024]{1,0:T(8,128)(2,1)}) custom-call(bf16[1024,512]{1,0:T(8,128)(2,1)} %bitcast.75, f32[8,512]{1,0:T(8,128)} %bias_ref.1, f32[8,512]{1,0:T(8,128)} %out_ref.1, f32[1024,128]{1,0:T(8,128)} %copy-done.1, ...), custom_call_target="tpu_custom_call" | custom-call | flops 1000000000 | bytes 8388608 | tf_op jit(solution)/shard_map/pallas_call | solution.py:238
  155.3 27.5 %all_to_all.52 = bf16[16,64,256]{2,1,0:T(8,128)(2,1)S(1)} all-to-all(bf16[16,64,256]{2,1,0:T(8,128)(2,1)} %bitcast.82), channel_id=1, replica_groups=mesh['dp'=16,'rule'=32] {'dp'}, dimensions={0} | all-to-all | bytes 1048576 | tf_op jit(solution)/shard_map/all_to_all | solution.py:366
  182.7 1.0 convolution_convert_fusion.1
  185.1 3.4 %all-to-all-start.3 = ((bf16[16,1,64]{2,1,0:T(2,128)(2,1)}), bf16[16,1,64]{2,1,0:T(2,128)(2,1)S(1)}, u32[]{:S(2)}, u32[]{:S(2)}) async-start(bf16[16,1,64]{2,1,0:T(2,128)(2,1)} %all_to_all.44), calls=%async_computation.3 | async-start | bytes 16384 | tf_op jit(solution)/shard_map/all_to_all | solution.py:372
  188.5 2.1 convolution_convert_fusion
  190.6 4.4 %all-to-all-done.3 = bf16[16,1,64]{2,1,0:T(2,128)(2,1)S(1)} async-done(((bf16[16,1,64]{2,1,0:T(2,128)(2,1)}), bf16[16,1,64]{2,1,0:T(2,128)(2,1)S(1)}, u32[]{:S(2)}, u32[]{:S(2)}) %all-to-all-start.3) | async-done | bytes 2080 | tf_op jit(solution)/shard_map/all_to_all | solution.py:372
  196.0 24.9 %all-gather.5.cloned.1.call-done = bf16[4096,256]{1,0:T(8,128)(2,1)} async-done(((bf16[256,256]{1,0:T(8,128)(2,1)}), bf16[4096,256]{1,0:T(8,128)(2,1)}) %all-gather.5.cloned.1.call-update) | async-done | bytes 2097168 | tf_op jit(solution)/shard_map/all_gather | solution.py:369
  220.8 5.9 %shard_map.123 = bf16[256,512]{1,0:T(8,128)(2,1)} custom-call(bf16[16,8,32,256]{3,2,1,0:T(8,128)(2,1)} %bitcast.77, bf16[4,8,512,128]{3,2,1,0:T(8,128)(2,1)} %bitcast.74), custom_call_target="tpu_custom_call" | custom-call | flops 1000000000 | bytes 6291456 | tf_op jit(solution)/shard_map/pallas_call | solution.py:280
  (35 shorter events, 4.3 us)
Async XLA Ops:
  7.9 0.9 copy-start.2
  8.9 0.9 copy-start.3
  11.6 26.9 %copy-start.9 = (bf16[4096,2]{0,1:T(2,128)(2,1)S(1)}, bf16[4096,2]{0,1:T(2,128)(2,1)}, u32[]{:S(2)}) copy-start(bf16[4096,2]{0,1:T(2,128)(2,1)} %param.12) | copy-start | bytes 49156
  11.6 26.9 %copy-start.7 = (s32[4096,2]{0,1:T(2,128)S(1)}, s32[4096,2]{0,1:T(2,128)}, u32[]{:S(2)}) copy-start(s32[4096,2]{0,1:T(2,128)} %param.11) | copy-start | bytes 98308
  11.6 26.9 %copy-start.8 = (s32[4096,2]{0,1:T(2,128)S(1)}, s32[4096,2]{0,1:T(2,128)}, u32[]{:S(2)}) copy-start(s32[4096,2]{0,1:T(2,128)} %param.10) | copy-start | bytes 98308
  14.2 49.3 %all-to-all-start = ((bf16[512,2,320]{2,1,0:T(2,128)(2,1)}), bf16[512,2,320]{2,1,0:T(2,128)(2,1)}, u32[]{:S(2)}, u32[]{:S(2)}) async-start(bf16[512,2,320]{2,1,0:T(2,128)(2,1)} %reshape.70), calls=%async_computation | async-start | bytes 1572864 | tf_op jit(solution)/shard_map/all_to_all | solution.py:330
  38.2 145.5 %all-gather.3.cloned.1.call-start = ((), (), s32[]{:S(2)}) async-start(), calls=%async_computation.5 | async-start | bytes 4325376 | tf_op jit(solution)/shard_map/all_gather | solution.py:354
  45.4 0.8 copy-start
  46.2 0.8 copy-start.1
  47.1 0.6 copy-start.4
  73.9 146.9 %all-gather.5.cloned.1.call-start = ((), (), s32[]{:S(2)}) async-start(), calls=%async_computation.6 | async-start | bytes 2228224 | tf_op jit(solution)/shard_map/all_gather | solution.py:369
  155.2 33.3 %copy-start.5 = (bf16[1024,512]{1,0:T(8,128)(2,1)S(1)}, bf16[1024,512]{1,0:T(8,128)(2,1)}, u32[]{:S(2)}) copy-start(bf16[1024,512]{1,0:T(8,128)(2,1)} %get-tuple-element.31) | copy-start | bytes 3145732
  155.2 33.3 %copy-start.6 = (bf16[1024,256]{1,0:T(8,128)(2,1)S(1)}, bf16[1024,256]{1,0:T(8,128)(2,1)}, u32[]{:S(2)}) copy-start(bf16[1024,256]{1,0:T(8,128)(2,1)} %get-tuple-element.30) | copy-start | bytes 1572868
  185.1 9.9 %all-to-all-start.3 = ((bf16[16,1,64]{2,1,0:T(2,128)(2,1)}), bf16[16,1,64]{2,1,0:T(2,128)(2,1)S(1)}, u32[]{:S(2)}, u32[]{:S(2)}) async-start(bf16[16,1,64]{2,1,0:T(2,128)(2,1)} %all_to_all.44), calls=%async_computation.3 | async-start | bytes 16384 | tf_op jit(solution)/shard_map/all_to_all | solution.py:372
Sparse Core Ops, SparseCore 0:
  74.1 91.4 all-gather.2
  183.9 36.9 all-gather.4

commit v5 on v2

--- a/solution.py
+++ b/solution.py
@@ -18,10 +18,10 @@
     return lax.dot_general(a, b, dims, preferred_element_type=F32)
 
 
-def tables_kernel(block, me_ref, owner_ref, pos_ref, cot_ref, sort_ref, unsort_ref, pick_ref, cot_out_ref):
+def tables_kernel(block, me_ref, owner_ref, pos_ref, cot_ref, lane_ref, row_ref, pick_ref, cot_out_ref):
     me = me_ref[0]
     groups, tokens = owner_ref.shape[1:]
-    rows = sort_ref.shape[0]
+    rows = cot_out_ref.shape[0]
     slots = 2 * (tokens // block)
     owner = [owner_ref[k] for k in range(2)]
     pos = [pos_ref[k] for k in range(2)]
@@ -53,7 +53,6 @@
     cot_total = jnp.zeros((rows, 128), F32)
     lane_row = lax.broadcasted_iota(jnp.int32, (128, tokens), 0)
     buffer_row = lax.broadcasted_iota(jnp.int32, (rows, 128), 0)
-    buffer_lane = lax.broadcasted_iota(jnp.int32, (128, rows), 1)
     for step in range(groups // pair):
         ones, highs, lows, cots = [], [], [], []
         for part in range(pair):
@@ -74,10 +73,9 @@
         at_row = (mm(chosen, high_row, NT) * 32.0 + mm(chosen, low_row, NT)).astype(jnp.int32) - 1
         cot_lane = mm(cot_row, chosen, NT).astype(BF16)
         hit = jnp.where(buffer_row == at_lane[0:1], 1.0, 0.0).astype(BF16)
-        sort_ref[:, step * 128 : (step + 1) * 128] = hit
+        lane_ref[:, step * 128 : (step + 1) * 128] = at_lane[0:8]
         cot_total = cot_total + mm(hit, cot_lane, NT)
-        at_row = jnp.concatenate([at_row] * (rows // 128), axis=1)
-        unsort_ref[step * 128 : (step + 1) * 128, :] = jnp.where(buffer_lane == at_row, 1.0, 0.0).astype(BF16)
+        row_ref[step * 128 : (step + 1) * 128, :] = at_row
     cot_out_ref[...] = cot_total
 
 
@@ -88,8 +86,8 @@
     return pl.pallas_call(
         functools.partial(tables_kernel, block),
         out_shape=(
-            jax.ShapeDtypeStruct((rows, received), BF16),
-            jax.ShapeDtypeStruct((received, rows), BF16),
+            jax.ShapeDtypeStruct((8, received), jnp.int32),
+            jax.ShapeDtypeStruct((received, 128), jnp.int32),
             jax.ShapeDtypeStruct((2, received, tokens), BF16),
             jax.ShapeDtypeStruct((rows, 128), F32),
         ),
@@ -100,24 +98,28 @@
     )(me, owner, pos, cot)
 
 
-def forward_kernel(sort_ref, got_ref, weight_ref, rows_ref, part_ref, attn_ref):
-    groups, height, features = got_ref.shape
-    slots = sort_ref.shape[1] // groups
-    got = got_ref[:, :slots].reshape(groups * slots, features)
-    rows = mm(sort_ref[...], got).astype(BF16)
+def forward_kernel(lane_ref, got_ref, weight_ref, rows_ref, part_ref, attn_ref, got):
+    features = got.shape[1]
+    capacity = rows_ref.shape[0]
+    slots = got.shape[0] // got_ref.shape[0]
+    block = attn_ref.shape[1]
+
+    @pl.when(pl.program_id(0) == 0)
+    def _():
+        got[...] = got_ref[:, :slots].reshape(got.shape)
+        attn_ref[:, :, :features] = got_ref[:, slots : slots + block]
+        attn_ref[:, :, features:] = got_ref[:, slots + block :]
+
+    row = lax.broadcasted_iota(jnp.int32, (capacity, got.shape[0]), 0)
+    hit = row == lane_ref[0:1] - pl.program_id(0) * capacity
+    rows = mm(jnp.where(hit, 1.0, 0.0).astype(BF16), got[...]).astype(BF16)
     rows_ref[...] = rows
     part_ref[...] = mm(rows, weight_ref[0]).astype(BF16)
 
-    @pl.when(pl.program_id(0) == 0)
-    def _():
-        block = attn_ref.shape[1]
-        attn_ref[:, :, :features] = got_ref[:, slots : slots + block]
-        attn_ref[:, :, features:] = got_ref[:, slots + block :]
-
-
-def forward(sort, got, weight):
+
+def forward(lane, got, weight, rows):
     adapters, features, hidden = weight.shape
-    rows, received = sort.shape
+    received = lane.shape[1]
     capacity = rows // adapters
     slots = received // got.shape[0]
     attn = (got.shape[0], (got.shape[1] - slots) // 2, 2 * features)
@@ -130,7 +132,7 @@
             jax.ShapeDtypeStruct(attn, BF16),
         ),
         in_specs=[
-            pl.BlockSpec((capacity, received), lambda a: (a, 0)),
+            pl.BlockSpec((8, received), lambda a: (0, 0)),
             pl.BlockSpec(got.shape, lambda a: (0, 0, 0)),
             pl.BlockSpec((1, features, hidden), lambda a: (a, 0, 0)),
         ],
@@ -139,14 +141,15 @@
             pl.BlockSpec((capacity, hidden), lambda a: (a, 0)),
             pl.BlockSpec(attn, lambda a: (0, 0, 0)),
         ),
-        compiler_params=pltpu.CompilerParams(vmem_limit_bytes=58 * 2**20),
+        scratch_shapes=[pltpu.VMEM((received, features), BF16)],
+        compiler_params=pltpu.CompilerParams(vmem_limit_bytes=12 * 2**20),
         cost_estimate=pl.CostEstimate(flops=10**9, bytes_accessed=6 * 2**20, transcendentals=0),
-    )(sort, got, weight)
+    )(lane, got, weight)
 
 
 def backward_kernel(
-    pre_ref, bias_ref, out_ref, cot_ref, weight_ref, unsort_ref,
-    half_ref, bias_grad_ref, out_grad_ref, back_ref, reward_ref, grads,
+    pre_ref, bias_ref, out_ref, cot_ref, weight_ref, row_ref,
+    half_ref, bias_grad_ref, out_grad_ref, back_ref, reward_ref, unsort, grads,
 ):
     a = pl.program_id(0)
     capacity, hidden = pre_ref.shape
@@ -166,18 +169,25 @@
     grads[at, :features] = mm(half, weight_ref[0], NT).astype(BF16)
     grads[at, features:] = jnp.broadcast_to(reward, (capacity, 128)).astype(BF16)
 
+    height = row_ref.shape[0]
+    part = pl.ds(pl.multiple_of(a * height, height), height)
+    lane = lax.broadcasted_iota(jnp.int32, (height, 128), 1)
+    for n in range(0, unsort.shape[1], 128):
+        hit = row_ref[...] - n == lane
+        unsort[part, n : n + 128] = jnp.where(hit, 1.0, 0.0).astype(BF16)
+
     @pl.when(a == pl.num_programs(0) - 1)
     def _():
-        back = mm(unsort_ref[...], grads[...]).astype(BF16)
+        back = mm(unsort[...], grads[...]).astype(BF16)
         back_ref[...] = back[:, :features]
         first = lax.broadcasted_iota(jnp.int32, (16, 128), 1) == 0
         first = jnp.where(first, 1.0, 0.0).astype(BF16)
         reward_ref[...] = mm(first, back[:, features:], NT).astype(BF16)
 
 
-def backward(pre, bias, read_out, cot, weight, unsort):
+def backward(pre, bias, read_out, cot, weight, row):
     adapters, features, hidden = weight.shape
-    received, rows = unsort.shape
+    received, rows = row.shape[0], pre.shape[0]
     capacity = rows // adapters
     line = pl.BlockSpec((1, 1, hidden), lambda a: (a, 0, 0))
     half, bias_grad, out_grad, back, reward = pl.pallas_call(
@@ -196,7 +206,7 @@
             line,
             pl.BlockSpec((capacity, 128), lambda a: (a, 0)),
             pl.BlockSpec((1, features, hidden), lambda a: (a, 0, 0)),
-            pl.BlockSpec((received, rows), lambda a: (0, 0)),
+            pl.BlockSpec((received // adapters, 128), lambda a: (a, 0)),
         ],
         out_specs=(
             pl.BlockSpec((capacity, hidden), lambda a: (a, 0)),
@@ -205,10 +215,13 @@
             pl.BlockSpec((received, features), lambda a: (0, 0)),
             pl.BlockSpec((16, received), lambda a: (0, 0)),
         ),
-        scratch_shapes=[pltpu.VMEM((rows, features + 128), BF16)],
-        compiler_params=pltpu.CompilerParams(vmem_limit_bytes=58 * 2**20),
+        scratch_shapes=[
+            pltpu.VMEM((received, rows), BF16),
+            pltpu.VMEM((rows, features + 128), BF16),
+        ],
+        compiler_params=pltpu.CompilerParams(vmem_limit_bytes=16 * 2**20),
         cost_estimate=pl.CostEstimate(flops=10**9, bytes_accessed=8 * 2**20, transcendentals=2**19),
-    )(pre, bias[:, None], read_out[:, None], cot, weight, unsort)
+    )(pre, bias[:, None], read_out[:, None], cot, weight, row)
     return half, bias_grad[:, 0], out_grad[:, 0], back, reward
 
 
@@ -261,15 +274,14 @@
     owner = rule_all // adapters
     pos = jnp.where(slot_all >= 0, rule_all % adapters * capacity + slot_all, -1)
     me = lax.axis_index("dp").astype(jnp.int32).reshape(1)
-    sort, unsort, pick, cot_rows = tables(block, rows, me, owner, pos, cot_all)
+    lane, row, pick, cot_rows = tables(block, rows, me, owner, pos, cot_all)
     (outgoing,) = call(
         pick_kernel, [((dp_size, slots + 2 * block, feature_cols), BF16)], 200, 2,
         pick, group_rows, attn_input,
     )
     got = lax.all_to_all(outgoing, "dp", split_axis=0, concat_axis=0, tiled=True)
-    rows_buf, partial_pre, attn_cols = forward(sort, got, adapter_in)
+    rows_buf, partial_pre, attn_cols = forward(lane, got, adapter_in, rows)
     attn_all = lax.all_gather(attn_cols, "rule", axis=1, tiled=True)
-    attn_all = attn_all.reshape(dp_size * tokens, -1)
     shares = lax.all_to_all(partial_pre, "rule", split_axis=0, concat_axis=0, tiled=True)
     share = jnp.sum(
         shares.reshape(rule_size, rows // rule_size, hidden_units).astype(F32), axis=0
@@ -278,12 +290,17 @@
     preact = lax.all_to_all(share, "rule", split_axis=0, concat_axis=0, tiled=True)
 
     grad_half, bias_grad, out_grad, back, reward = backward(
-        preact, adapter_bias, adapter_out, cot_rows, adapter_in, unsort
+        preact, adapter_bias, adapter_out, cot_rows, adapter_in, row
     )
     returned = lax.all_to_all(back, "dp", split_axis=0, concat_axis=0, tiled=True)
     state_grad = mm(pick[0] + pick[1], returned, TN).astype(BF16)
     attn_all, state_grad = lax.optimization_barrier((attn_all, state_grad))
-    state_all = lax.all_gather(state_grad, "dp", axis=0, tiled=True)
+    cut = tokens // 2 - 8
+    width = attn_all.shape[2]
+    attn_low = attn_all[:, :cut].reshape(dp_size * cut, width)
+    attn_high = attn_all[:, cut:].reshape(dp_size * (tokens - cut), width)
+    state_low = lax.all_gather(state_grad[:cut], "dp", axis=0, tiled=True)
+    state_high = lax.all_gather(state_grad[cut:], "dp", axis=0, tiled=True)
 
     reward_back = lax.all_to_all(
         reward[0].reshape(dp_size, slots), "dp", split_axis=0, concat_axis=0, tiled=True
@@ -298,7 +315,8 @@
         grad_half.reshape(adapters, capacity, hidden_units),
         preferred_element_type=F32,
     ).astype(BF16)
-    o_proj_grad = mm(state_all, attn_all, TN).astype(BF16)
+    o_proj_grad = mm(state_low, attn_low, TN) + mm(state_high, attn_high, TN)
+    o_proj_grad = o_proj_grad.astype(BF16)
     return (rewards, in_grad, bias_grad, out_grad, o_proj_grad)
 
 

time: 228 us -> 217 us (0.952)
  waiting for transfers between devices: 52.8 us -> 34.1 us
  blocking collectives: 94.3 us -> 110 us
  Pallas kernels: 21.9 us -> 12.2 us
  local copies, waits for them, and re-layouts: 10.3 us -> 13.8 us
    all_gather x1, waiting for transfers between devices: 23.5 us -> 1.57 us  [local(): state_high = lax.all_gather(state_grad[cut:], 'dp', axis=0, tiled=True)]
    all_gather x0 -> x1, blocking collectives: none -> 18.8 us  [local(): state_low = lax.all_gather(state_grad[:cut], 'dp', axis=0, tiled=True)]
    pallas_call x1, Pallas kernels: 9.39 us -> 4 us  [backward(): pl.pallas_call(backward_kernel, grid=(adapters,), out_shape=(jax.ShapeDty...]
    unnamed x24 -> x30, local copies, waits for them, and re-layouts: 5.85 us -> 9.86 us
    pallas_call x1, Pallas kernels: 7.73 us -> 3.9 us  [forward(): pl.pallas_call(forward_kernel, grid=(adapters,), out_shape=(jax.ShapeDtyp...]
    dot_general x2 -> x3, matrix products: 5.85 us -> 3.88 us  [mm(): return lax.dot_general(a, b, dims, preferred_element_type=F32)]
  transfers between devices with their start and end apart: 5 -> 5, of which waited for: 3 -> 4; matrix products, arithmetic and copies ran while one was open for 4% -> 4% of each run, Pallas kernels for 6% -> 4%
where the time goes in v5:
time: 217 us; the launch traced here: 216 us
  blocking collectives  110 us (51%)
  waiting for transfers between devices  34.1 us (16%)
  starting transfers between devices  24.5 us (11%)
  between operations  14.2 us (7%)
  local copies, waits for them, and re-layouts  13.8 us (6%)
  Pallas kernels  12.2 us (6%)
  matrix products  6.19 us (3%)
    all_to_all x1, blocking collectives, local(): lax.all_to_all(partial_pre, 'rule', split_axis=0, concat_axis=0, tiled=True)  36.2 us
    all_to_all x1, blocking collectives, local(): lax.all_to_all(outgoing, 'dp', split_axis=0, concat_axis=0, tiled=True)  29.2 us
    all_to_all x1, waiting for transfers between devices, local(): lax.all_to_all(share, 'rule', split_axis=0, concat_axis=0, tiled=True)  26.6 us
    all_to_all x1, blocking collectives, local(): lax.all_to_all(back, 'dp', split_axis=0, concat_axis=0, tiled=True)  26.1 us
    all_gather x1, blocking collectives, local(): state_low = lax.all_gather(state_grad[:cut], 'dp', axis=0, tiled=True)  18.8 us
    all_to_all x1, starting transfers between devices, local(): lax.all_to_all(hidden_states, 'rule', split_axis=1, concat_axis=0, tiled=...  13.9 us
    unnamed x30, local copies, waits for them, and re-layouts  9.86 us
    all_to_all x1, starting transfers between devices, local(): lax.all_to_all(share, 'rule', split_axis=0, concat_axis=0, tiled=True)  7.21 us
  transfers between devices with their start and end apart: 5, of which 4 were waited for; matrix products, arithmetic and copies ran while one was open for 4% of the time, Pallas kernels for 4%

profile of v5, /device:TPU:1, one launch (start us, length us, event | category | flops | bytes accessed | tf_op | source)
XLA Modules:
  0.0 216.3 jit_solution(194178322490480840)
XLA Ops:
  7.2 13.9 %all-to-all-start = ((bf16[8,32,256]{2,0,1:T(8,128)(2,1)}), bf16[8,32,256]{2,0,1:T(8,128)(2,1)S(1)}, u32[]{:S(2)}, u32[]{:S(2)}) async-start(bf16[8,32,256]{2,0,1:T(8,128)(2,1)} %bitcast.87), calls=%async_computation | async-start | bytes 262144 | tf_op jit(solution)/shard_map/all_to_all | solution.py:269
  21.8 0.8 fusion.7
  22.6 4.0 %shard_map.119 = (s32[8,1024]{1,0:T(8,128)S(1)}, s32[1024,128]{1,0:T(8,128)S(1)}, bf16[2,1024,256]{2,1,0:T(8,128)(2,1)S(1)}, f32[1024,128]{1,0:T(8,128)S(1)}) custom-call(s32[1]{0:T(128)} %bitcast.me_ref, s32[2,16,256]{2,1,0:T(8,128)S(1)} %get-tuple-element.34.owner_ref, s32[2,16,256]{2,1,0:T(8,128)S(1)} %get-tuple-element.33.pos_ref, ...), custom_call_target="tpu_custom_call" | custom-call | flops 1000000000 | bytes 6291456 | tf_op jit(solution)/shard_map/pallas_call | solution.py:86
  27.4 0.8 copy-done.7
  28.2 2.0 all-to-all-done
  30.5 29.2 %all_to_all.63.got_ref = bf16[16,80,256]{2,1,0:T(8,128)(2,1)S(1)} all-to-all(bf16[16,80,256]{2,1,0:T(8,128)(2,1)S(1)} %shard_map.120), channel_id=1, replica_groups=mesh['dp'=16,'rule'=32] {'dp'}, dimensions={0} | all-to-all | bytes 1310720 | tf_op jit(solution)/shard_map/all_to_all | solution.py:282
  59.7 3.9 %shard_map.121 = (bf16[1024,256]{1,0:T(8,128)(2,1)S(1)}, bf16[1024,512]{1,0:T(8,128)(2,1)S(1)}, bf16[16,8,512]{2,1,0:T(8,128)(2,1)}) custom-call(s32[8,1024]{1,0:T(8,128)S(1)} %get-tuple-element.20.lane_ref, bf16[16,80,256]{2,1,0:T(8,128)(2,1)S(1)} %all_to_all.63.got_ref, bf16[8,256,512]{2,1,0:T(8,128)(2,1)S(1)} %copy-done), custom_call_target="tpu_custom_call" | custom-call | flops 1000000000 | bytes 6291456 | tf_op jit(solution)/shard_map/pallas_call | solution.py:126
  63.6 1.0 copy-done.2
  65.4 36.2 %all_to_all.64 = bf16[32,32,512]{2,1,0:T(8,128)(2,1)S(1)} all-to-all(bf16[32,32,512]{2,1,0:T(8,128)(2,1)} %bitcast.79), channel_id=1, replica_groups=mesh['dp'=16,'rule'=32] {'rule'}, dimensions={0} | all-to-all | bytes 2097152 | tf_op jit(solution)/shard_map/all_to_all | solution.py:285
  101.8 1.1 broadcast_in_dim.14
  102.9 7.2 %all-to-all-start.3 = ((bf16[32,32,512]{2,1,0:T(8,128)(2,1)}), bf16[32,32,512]{2,1,0:T(8,128)(2,1)S(1)}, u32[]{:S(2)}, u32[]{:S(2)}) async-start(bf16[32,32,512]{2,1,0:T(8,128)(2,1)} %broadcast_in_dim.14), calls=%async_computation.3 | async-start | bytes 2097152 | tf_op jit(solution)/shard_map/all_to_all | solution.py:290
  110.2 26.6 %all-to-all-done.3 = bf16[32,32,512]{2,1,0:T(8,128)(2,1)S(1)} async-done(((bf16[32,32,512]{2,1,0:T(8,128)(2,1)}), bf16[32,32,512]{2,1,0:T(8,128)(2,1)S(1)}, u32[]{:S(2)}, u32[]{:S(2)}) %all-to-all-start.3) | async-done | bytes 1048608 | tf_op jit(solution)/shard_map/all_to_all | solution.py:290
  136.9 1.6 copy-done.1
  138.5 1.0 copy-done.6
  139.6 1.0 copy-done.8
  140.6 4.0 %shard_map.122 = (bf16[1024,512]{1,0:T(8,128)(2,1)S(1)}, f32[8,1,512]{2,1,0:T(1,128)S(1)}, f32[8,1,512]{2,1,0:T(1,128)S(1)}, bf16[1024,256]{1,0:T(8,128)(2,1)S(1)}, bf16[16,1024]{1,0:T(8,128)(2,1)S(1)}) custom-call(bf16[1024,512]{1,0:T(8,128)(2,1)S(1)} %bitcast.77, f32[8,1,512]{2,1,0:T(1,128)S(1)} %broadcast_in_dim.15.bias_ref, ...), custom_call_target="tpu_custom_call" | custom-call | flops 1000000000 | bytes 8388608 | tf_op jit(solution)/shard_map/pallas_call | solution.py:193
  144.6 26.1 %all_to_all.65 = bf16[16,64,256]{2,1,0:T(8,128)(2,1)S(1)} all-to-all(bf16[16,64,256]{2,1,0:T(8,128)(2,1)S(1)} %bitcast.81), channel_id=1, replica_groups=mesh['dp'=16,'rule'=32] {'dp'}, dimensions={0} | all-to-all | bytes 1048576 | tf_op jit(solution)/shard_map/all_to_all | solution.py:295
  172.5 3.3 %all-to-all-start.4 = ((bf16[16,1,64]{2,1,0:T(2,128)(2,1)}), bf16[16,1,64]{2,1,0:T(2,128)(2,1)S(1)}, u32[]{:S(2)}, u32[]{:S(2)}) async-start(bf16[16,1,64]{2,1,0:T(2,128)(2,1)} %all_to_all.56), calls=%async_computation.4 | async-start | bytes 16384 | tf_op jit(solution)/shard_map/all_to_all | solution.py:305
  175.9 2.1 convolution_convert_fusion
  178.5 3.9 %all-to-all-done.4 = bf16[16,1,64]{2,1,0:T(2,128)(2,1)S(1)} async-done(((bf16[16,1,64]{2,1,0:T(2,128)(2,1)}), bf16[16,1,64]{2,1,0:T(2,128)(2,1)S(1)}, u32[]{:S(2)}, u32[]{:S(2)}) %all-to-all-start.4) | async-done | bytes 2080 | tf_op jit(solution)/shard_map/all_to_all | solution.py:305
  183.4 1.4 copy-done.10
  185.6 18.8 %all_gather.10 = bf16[1920,256]{1,0:T(8,128)(2,1)S(1)} all-gather(bf16[120,256]{1,0:T(8,128)(2,1)S(1)} %slice-done.1), channel_id=1, replica_groups=mesh['dp'=16,'rule'=32] {'dp'}, dimensions={0}, use_global_device_ids=true | all-gather | bytes 1044480 | tf_op jit(solution)/shard_map/all_gather | solution.py:302
  205.2 1.6 all-gather.5.cloned.1.call-done
  206.8 2.7 %fusion = bf16[256,512]{1,0:T(8,128)(2,1)} fusion(f32[256,512]{1,0:T(8,128)S(1)} %fusion.13, bf16[2176,256]{1,0:T(8,128)(2,1)} %all-gather.5.cloned.1.call-done, bf16[2176,512]{1,0:T(8,128)(2,1)S(1)} %bitcast.85), kind=kOutput, calls=%fused_computation.2 | convolution fusion | flops 570687488 | bytes 4128768 | tf_op jit(solution)/shard_map/dot_general | solution.py:18
  (47 shorter events, 7.8 us)
Async XLA Ops:
  7.2 23.0 %copy-start.9 = (bf16[8,8192]{1,0:T(8,128)(2,1)S(1)}, bf16[8,8192]{1,0:T(8,128)(2,1)}, u32[]{:S(2)}) copy-start(bf16[8,8192]{1,0:T(8,128)(2,1)} %attn_ref.1) | copy-start | bytes 393220
  7.2 23.0 %all-to-all-start = ((bf16[8,32,256]{2,0,1:T(8,128)(2,1)}), bf16[8,32,256]{2,0,1:T(8,128)(2,1)S(1)}, u32[]{:S(2)}, u32[]{:S(2)}) async-start(bf16[8,32,256]{2,0,1:T(8,128)(2,1)} %bitcast.87), calls=%async_computation | async-start | bytes 262144 | tf_op jit(solution)/shard_map/all_to_all | solution.py:269
  21.0 150.1 %all-gather.3.cloned.1.call-start = ((), (), s32[]{:S(2)}) async-start(), calls=%async_computation.6 | async-start | bytes 4325376 | tf_op jit(solution)/shard_map/all_gather | solution.py:284
  26.6 0.8 copy-start.5
  27.4 0.8 copy-start.7
  28.2 31.5 %copy-start = (bf16[8,256,512]{2,1,0:T(8,128)(2,1)S(1)}, bf16[8,256,512]{2,1,0:T(8,128)(2,1)}, u32[]{:S(2)}) copy-start(bf16[8,256,512]{2,1,0:T(8,128)(2,1)} %weight_ref.3) | copy-start | bytes 6291460
  63.6 1.0 copy-start.2
  64.6 0.8 copy-start.3
  101.7 8.5 %copy-start.12 = (f32[8,512]{1,0:T(8,128)S(1)}, f32[8,512]{1,0:T(8,128)}, u32[]{:S(2)}) copy-start(f32[8,512]{1,0:T(8,128)} %param.14) | copy-start | bytes 49156
  101.7 8.6 %copy-start.13 = (f32[8,512]{1,0:T(8,128)S(1)}, f32[8,512]{1,0:T(8,128)}, u32[]{:S(2)}) copy-start(f32[8,512]{1,0:T(8,128)} %param.15) | copy-start | bytes 49156
  102.9 34.0 %all-to-all-start.3 = ((bf16[32,32,512]{2,1,0:T(8,128)(2,1)}), bf16[32,32,512]{2,1,0:T(8,128)(2,1)S(1)}, u32[]{:S(2)}, u32[]{:S(2)}) async-start(bf16[32,32,512]{2,1,0:T(8,128)(2,1)} %broadcast_in_dim.14), calls=%async_computation.3 | async-start | bytes 2097152 | tf_op jit(solution)/shard_map/all_to_all | solution.py:290
  110.1 96.6 %all-gather.5.cloned.1.call-start = ((), (), s32[]{:S(2)}) async-start(), calls=%async_computation.7 | async-start | bytes 1183744 | tf_op jit(solution)/shard_map/all_gather | solution.py:303
  136.9 1.6 copy-start.1
  138.5 1.0 copy-start.6
  139.6 1.0 copy-start.8
  144.6 31.3 %copy-start.4 = (bf16[1024,256]{1,0:T(8,128)(2,1)S(1)}, bf16[1024,256]{1,0:T(8,128)(2,1)}, u32[]{:S(2)}) copy-start(bf16[1024,256]{1,0:T(8,128)(2,1)} %copy-done.3) | copy-start | bytes 1572868
  171.1 12.3 %copy-start.11 = (bf16[256,256]{1,0:T(8,128)(2,1)}, bf16[256,256]{1,0:T(8,128)(2,1)S(1)}, u32[]{:S(2)}) copy-start(bf16[256,256]{1,0:T(8,128)(2,1)S(1)} %convolution_convert_fusion.1) | copy-start | bytes 393220
  172.5 9.9 %all-to-all-start.4 = ((bf16[16,1,64]{2,1,0:T(2,128)(2,1)}), bf16[16,1,64]{2,1,0:T(2,128)(2,1)S(1)}, u32[]{:S(2)}, u32[]{:S(2)}) async-start(bf16[16,1,64]{2,1,0:T(2,128)(2,1)} %all_to_all.56), calls=%async_computation.4 | async-start | bytes 16384 | tf_op jit(solution)/shard_map/all_to_all | solution.py:305
  182.6 2.2 %copy-start.10 = (bf16[16,256,512]{2,1,0:T(8,128)(2,1)S(1)}, bf16[16,256,512]{2,1,0:T(8,128)(2,1)}, u32[]{:S(2)}) copy-start(bf16[16,256,512]{2,1,0:T(8,128)(2,1)} %all-gather.3.cloned.1.call-done) | copy-start | bytes 12582916
  184.8 0.8 slice-start.1
  184.8 19.7 %slice-start = ((bf16[16,256,512]{2,1,0:T(8,128)(2,1)}), bf16[16,120,512]{2,1,0:T(8,128)(2,1)S(1)}, s32[]{:S(2)}) async-start(bf16[16,256,512]{2,1,0:T(8,128)(2,1)} %all-gather.3.cloned.1.call-done), calls=%async_computation.8 | async-start | bytes 3932160 | tf_op jit(solution)/shard_map/slice | solution.py:300
Sparse Core Ops, SparseCore 0:
  65.5 98.1 all-gather.2
  171.9 34.7 all-gather.4

commit v6 on v5

--- a/solution.py
+++ b/solution.py
@@ -18,7 +18,7 @@
     return lax.dot_general(a, b, dims, preferred_element_type=F32)
 
 
-def tables_kernel(block, me_ref, owner_ref, pos_ref, cot_ref, lane_ref, row_ref, pick_ref, cot_out_ref):
+def tables_kernel(block, me_ref, owner_ref, pos_ref, cot_ref, lane_ref, pick_ref, cot_out_ref):
     me = me_ref[0]
     groups, tokens = owner_ref.shape[1:]
     rows = cot_out_ref.shape[0]
@@ -70,13 +70,11 @@
         low_row = jnp.broadcast_to(jnp.concatenate(lows, axis=1), (128, wide))
         cot_row = jnp.broadcast_to(jnp.concatenate(cots, axis=1), (128, wide))
         at_lane = (mm(high_row, chosen, NT) * 32.0 + mm(low_row, chosen, NT)).astype(jnp.int32) - 1
-        at_row = (mm(chosen, high_row, NT) * 32.0 + mm(chosen, low_row, NT)).astype(jnp.int32) - 1
         cot_lane = mm(cot_row, chosen, NT).astype(BF16)
         hit = jnp.where(buffer_row == at_lane[0:1], 1.0, 0.0).astype(BF16)
         lane_ref[:, step * 128 : (step + 1) * 128] = at_lane[0:8]
         cot_total = cot_total + mm(hit, cot_lane, NT)
-        row_ref[step * 128 : (step + 1) * 128, :] = at_row
-    cot_out_ref[...] = cot_total
+    cot_out_ref[...] = cot_total.astype(BF16)
 
 
 def tables(block, rows, me, owner, pos, cot):
@@ -87,12 +85,11 @@
         functools.partial(tables_kernel, block),
         out_shape=(
             jax.ShapeDtypeStruct((8, received), jnp.int32),
-            jax.ShapeDtypeStruct((received, 128), jnp.int32),
             jax.ShapeDtypeStruct((2, received, tokens), BF16),
-            jax.ShapeDtypeStruct((rows, 128), F32),
+            jax.ShapeDtypeStruct((rows, 128), BF16),
         ),
         in_specs=[pl.BlockSpec(memory_space=pltpu.SMEM), vmem, vmem, vmem],
-        out_specs=(vmem, vmem, vmem, vmem),
+        out_specs=(vmem, vmem, vmem),
         compiler_params=pltpu.CompilerParams(vmem_limit_bytes=16 * 2**20),
         cost_estimate=pl.CostEstimate(flops=10**9, bytes_accessed=6 * 2**20, transcendentals=0),
     )(me, owner, pos, cot)
@@ -148,7 +145,7 @@
 
 
 def backward_kernel(
-    pre_ref, bias_ref, out_ref, cot_ref, weight_ref, row_ref,
+    pre_ref, bias_ref, out_ref, cot_ref, weight_ref, lane_ref,
     half_ref, bias_grad_ref, out_grad_ref, back_ref, reward_ref, unsort, grads,
 ):
     a = pl.program_id(0)
@@ -157,7 +154,7 @@
     read_out = out_ref[0]
     pre = pre_ref[...].astype(F32) + bias_ref[0]
     s = 1.0 / (1.0 + jnp.exp(-pre))
-    cot = jnp.concatenate([cot_ref[...]] * (hidden // 128), axis=1)
+    cot = jnp.concatenate([cot_ref[...].astype(F32)] * (hidden // 128), axis=1)
     activated = pre * s
     grad_pre = cot * read_out * s * (1.0 + pre * (1.0 - s))
     half = grad_pre.astype(BF16)
@@ -169,12 +166,17 @@
     grads[at, :features] = mm(half, weight_ref[0], NT).astype(BF16)
     grads[at, features:] = jnp.broadcast_to(reward, (capacity, 128)).astype(BF16)
 
-    height = row_ref.shape[0]
-    part = pl.ds(pl.multiple_of(a * height, height), height)
-    lane = lax.broadcasted_iota(jnp.int32, (height, 128), 1)
+    place = jnp.broadcast_to(lane_ref[0:1] + 1, (128, 128))
+    lane = lax.broadcasted_iota(jnp.int32, (128, 128), 1)
+    diagonal = lax.broadcasted_iota(jnp.int32, (128, 128), 0) == lane
+    diagonal = jnp.where(diagonal, 1.0, 0.0).astype(BF16)
+    high = (place // 32).astype(F32).astype(BF16)
+    low = (place % 32).astype(F32).astype(BF16)
+    row = mm(diagonal, high, NT) * 32.0 + mm(diagonal, low, NT)
+    row = row.astype(jnp.int32) - 1
+    part = pl.ds(pl.multiple_of(a * 128, 128), 128)
     for n in range(0, unsort.shape[1], 128):
-        hit = row_ref[...] - n == lane
-        unsort[part, n : n + 128] = jnp.where(hit, 1.0, 0.0).astype(BF16)
+        unsort[part, n : n + 128] = jnp.where(row - n == lane, 1.0, 0.0).astype(BF16)
 
     @pl.when(a == pl.num_programs(0) - 1)
     def _():
@@ -185,9 +187,9 @@
         reward_ref[...] = mm(first, back[:, features:], NT).astype(BF16)
 
 
-def backward(pre, bias, read_out, cot, weight, row):
+def backward(pre, bias, read_out, cot, weight, lane):
     adapters, features, hidden = weight.shape
-    received, rows = row.shape[0], pre.shape[0]
+    received, rows = lane.shape[1], pre.shape[0]
     capacity = rows // adapters
     line = pl.BlockSpec((1, 1, hidden), lambda a: (a, 0, 0))
     half, bias_grad, out_grad, back, reward = pl.pallas_call(
@@ -206,7 +208,7 @@
             line,
             pl.BlockSpec((capacity, 128), lambda a: (a, 0)),
             pl.BlockSpec((1, features, hidden), lambda a: (a, 0, 0)),
-            pl.BlockSpec((received // adapters, 128), lambda a: (a, 0)),
+            pl.BlockSpec((8, 128), lambda a: (0, a)),
         ],
         out_specs=(
             pl.BlockSpec((capacity, hidden), lambda a: (a, 0)),
@@ -221,7 +223,7 @@
         ],
         compiler_params=pltpu.CompilerParams(vmem_limit_bytes=16 * 2**20),
         cost_estimate=pl.CostEstimate(flops=10**9, bytes_accessed=8 * 2**20, transcendentals=2**19),
-    )(pre, bias[:, None], read_out[:, None], cot, weight, row)
+    )(pre, bias[:, None], read_out[:, None], cot, weight, lane)
     return half, bias_grad[:, 0], out_grad[:, 0], back, reward
 
 
@@ -274,7 +276,7 @@
     owner = rule_all // adapters
     pos = jnp.where(slot_all >= 0, rule_all % adapters * capacity + slot_all, -1)
     me = lax.axis_index("dp").astype(jnp.int32).reshape(1)
-    lane, row, pick, cot_rows = tables(block, rows, me, owner, pos, cot_all)
+    lane, pick, cot_rows = tables(block, rows, me, owner, pos, cot_all)
     (outgoing,) = call(
         pick_kernel, [((dp_size, slots + 2 * block, feature_cols), BF16)], 200, 2,
         pick, group_rows, attn_input,
@@ -290,7 +292,7 @@
     preact = lax.all_to_all(share, "rule", split_axis=0, concat_axis=0, tiled=True)
 
     grad_half, bias_grad, out_grad, back, reward = backward(
-        preact, adapter_bias, adapter_out, cot_rows, adapter_in, row
+        preact, adapter_bias, adapter_out, cot_rows, adapter_in, lane
     )
     returned = lax.all_to_all(back, "dp", split_axis=0, concat_axis=0, tiled=True)
     state_grad = mm(pick[0] + pick[1], returned, TN).astype(BF16)

time: 217 us -> 213 us (0.982)
  local copies, waits for them, and re-layouts: 13.8 us -> 9.16 us
  waiting for transfers between devices: 34.1 us -> 36.8 us
    unnamed x30 -> x20, local copies, waits for them, and re-layouts: 9.86 us -> 5.2 us
    all_to_all x1, blocking collectives: 36.2 us -> 33.9 us  [local(): lax.all_to_all(partial_pre, 'rule', split_axis=0, concat_axis=0, tiled=True)]
where the time goes in v6:
time: 213 us; the launch traced here: 212 us
  blocking collectives  108 us (51%)
  waiting for transfers between devices  36.8 us (17%)
  starting transfers between devices  24.5 us (12%)
  between operations  14.2 us (7%)
  Pallas kernels  12.3 us (6%)
  local copies, waits for them, and re-layouts  9.16 us (4%)
  matrix products  6.18 us (3%)
    all_to_all x1, blocking collectives, local(): lax.all_to_all(partial_pre, 'rule', split_axis=0, concat_axis=0, tiled=True)  33.9 us
    all_to_all x1, blocking collectives, local(): lax.all_to_all(outgoing, 'dp', split_axis=0, concat_axis=0, tiled=True)  29.3 us
    all_to_all x1, waiting for transfers between devices, local(): lax.all_to_all(share, 'rule', split_axis=0, concat_axis=0, tiled=True)  26.6 us
    all_to_all x1, blocking collectives, local(): lax.all_to_all(back, 'dp', split_axis=0, concat_axis=0, tiled=True)  26.1 us
    all_gather x1, blocking collectives, local(): state_low = lax.all_gather(state_grad[:cut], 'dp', axis=0, tiled=True)  18.7 us
    all_to_all x1, starting transfers between devices, local(): lax.all_to_all(hidden_states, 'rule', split_axis=1, concat_axis=0, tiled=...  13.9 us
    all_to_all x1, starting transfers between devices, local(): lax.all_to_all(share, 'rule', split_axis=0, concat_axis=0, tiled=True)  7.17 us
    unnamed x20, local copies, waits for them, and re-layouts  5.2 us
  transfers between devices with their start and end apart: 5, of which 4 were waited for; matrix products, arithmetic and copies ran while one was open for 4% of the time, Pallas kernels for 4%

profile of v6, /device:TPU:1, one launch (start us, length us, event | category | flops | bytes accessed | tf_op | source)
XLA Modules:
  0.0 212.1 jit_solution(8637694590641238099)
XLA Ops:
  7.2 13.9 %all-to-all-start = ((bf16[8,32,256]{2,0,1:T(8,128)(2,1)}), bf16[8,32,256]{2,0,1:T(8,128)(2,1)S(1)}, u32[]{:S(2)}, u32[]{:S(2)}) async-start(bf16[8,32,256]{2,0,1:T(8,128)(2,1)} %bitcast.87), calls=%async_computation | async-start | bytes 262144 | tf_op jit(solution)/shard_map/all_to_all | solution.py:271
  21.1 0.7 copy.51
  21.8 0.8 fusion.7
  22.6 3.5 %shard_map.119 = (s32[8,1024]{1,0:T(8,128)S(1)}, bf16[2,1024,256]{2,1,0:T(8,128)(2,1)S(1)}, bf16[1024,128]{1,0:T(8,128)(2,1)S(1)}) custom-call(s32[1]{0:T(128)} %bitcast.me_ref, s32[2,16,256]{2,1,0:T(8,128)S(1)} %get-tuple-element.32.owner_ref, s32[2,16,256]{2,1,0:T(8,128)S(1)} %get-tuple-element.31.pos_ref, bf16[2,16,256]{2,1,0:T(8,128)(2,1)S(1)} %bitcast.83), custom_call_target="tpu_custom_call" | custom-call | flops 1000000000 | bytes 6291456 | tf_op jit(solution)/shard_map/pallas_call | solution.py:84
  26.1 4.1 %all-to-all-done = bf16[8,32,256]{2,0,1:T(8,128)(2,1)S(1)} async-done(((bf16[8,32,256]{2,0,1:T(8,128)(2,1)}), bf16[8,32,256]{2,0,1:T(8,128)(2,1)S(1)}, u32[]{:S(2)}, u32[]{:S(2)}) %all-to-all-start) | async-done | bytes 131104 | tf_op jit(solution)/shard_map/all_to_all | solution.py:271
  30.5 29.3 %all_to_all.63.got_ref = bf16[16,80,256]{2,1,0:T(8,128)(2,1)S(1)} all-to-all(bf16[16,80,256]{2,1,0:T(8,128)(2,1)S(1)} %shard_map.120), channel_id=1, replica_groups=mesh['dp'=16,'rule'=32] {'dp'}, dimensions={0} | all-to-all | bytes 1310720 | tf_op jit(solution)/shard_map/all_to_all | solution.py:284
  59.8 3.9 %shard_map.121 = (bf16[1024,256]{1,0:T(8,128)(2,1)S(1)}, bf16[1024,512]{1,0:T(8,128)(2,1)S(1)}, bf16[16,8,512]{2,1,0:T(8,128)(2,1)}) custom-call(s32[8,1024]{1,0:T(8,128)S(1)} %get-tuple-element.19.lane_ref, bf16[16,80,256]{2,1,0:T(8,128)(2,1)S(1)} %all_to_all.63.got_ref, bf16[8,256,512]{2,1,0:T(8,128)(2,1)S(1)} %copy-done.3), custom_call_target="tpu_custom_call" | custom-call | flops 1000000000 | bytes 6291456 | tf_op jit(solution)/shard_map/pallas_call | solution.py:123
  63.7 0.8 copy-done
  64.6 33.9 %all_to_all.64 = bf16[32,32,512]{2,1,0:T(8,128)(2,1)S(1)} all-to-all(bf16[32,32,512]{2,1,0:T(8,128)(2,1)S(1)} %bitcast.79), channel_id=1, replica_groups=mesh['dp'=16,'rule'=32] {'rule'}, dimensions={0} | all-to-all | bytes 2097152 | tf_op jit(solution)/shard_map/all_to_all | solution.py:287
  98.7 1.1 broadcast_in_dim.14
  99.8 7.2 %all-to-all-start.3 = ((bf16[32,32,512]{2,1,0:T(8,128)(2,1)}), bf16[32,32,512]{2,1,0:T(8,128)(2,1)S(1)}, u32[]{:S(2)}, u32[]{:S(2)}) async-start(bf16[32,32,512]{2,1,0:T(8,128)(2,1)} %broadcast_in_dim.14), calls=%async_computation.3 | async-start | bytes 2097152 | tf_op jit(solution)/shard_map/all_to_all | solution.py:292
  107.0 26.6 %all-to-all-done.3 = bf16[32,32,512]{2,1,0:T(8,128)(2,1)S(1)} async-done(((bf16[32,32,512]{2,1,0:T(8,128)(2,1)}), bf16[32,32,512]{2,1,0:T(8,128)(2,1)S(1)}, u32[]{:S(2)}, u32[]{:S(2)}) %all-to-all-start.3) | async-done | bytes 1048608 | tf_op jit(solution)/shard_map/all_to_all | solution.py:292
  133.7 1.6 copy-done.4
  135.3 4.5 %shard_map.122 = (bf16[1024,512]{1,0:T(8,128)(2,1)S(1)}, f32[8,1,512]{2,1,0:T(1,128)S(1)}, f32[8,1,512]{2,1,0:T(1,128)S(1)}, bf16[1024,256]{1,0:T(8,128)(2,1)S(1)}, bf16[16,1024]{1,0:T(8,128)(2,1)S(1)}) custom-call(bf16[1024,512]{1,0:T(8,128)(2,1)S(1)} %bitcast.78, f32[8,1,512]{2,1,0:T(1,128)S(1)} %broadcast_in_dim.15.bias_ref, ...), custom_call_target="tpu_custom_call" | custom-call | flops 1000000000 | bytes 8388608 | tf_op jit(solution)/shard_map/pallas_call | solution.py:195
  139.8 26.1 %all_to_all.65 = bf16[16,64,256]{2,1,0:T(8,128)(2,1)S(1)} all-to-all(bf16[16,64,256]{2,1,0:T(8,128)(2,1)S(1)} %bitcast.81), channel_id=1, replica_groups=mesh['dp'=16,'rule'=32] {'dp'}, dimensions={0} | all-to-all | bytes 1048576 | tf_op jit(solution)/shard_map/all_to_all | solution.py:297
  167.1 0.7 all_to_all.56
  167.8 3.3 %all-to-all-start.4 = ((bf16[16,1,64]{2,1,0:T(2,128)(2,1)}), bf16[16,1,64]{2,1,0:T(2,128)(2,1)S(1)}, u32[]{:S(2)}, u32[]{:S(2)}) async-start(bf16[16,1,64]{2,1,0:T(2,128)(2,1)} %all_to_all.56), calls=%async_computation.4 | async-start | bytes 16384 | tf_op jit(solution)/shard_map/all_to_all | solution.py:307
  171.1 2.1 convolution_convert_fusion
  173.8 3.9 %all-to-all-done.4 = bf16[16,1,64]{2,1,0:T(2,128)(2,1)S(1)} async-done(((bf16[16,1,64]{2,1,0:T(2,128)(2,1)}), bf16[16,1,64]{2,1,0:T(2,128)(2,1)S(1)}, u32[]{:S(2)}, u32[]{:S(2)}) %all-to-all-start.4) | async-done | bytes 2080 | tf_op jit(solution)/shard_map/all_to_all | solution.py:307
  178.6 1.4 copy-done.5
  180.9 18.7 %all_gather.10 = bf16[1920,256]{1,0:T(8,128)(2,1)S(1)} all-gather(bf16[120,256]{1,0:T(8,128)(2,1)S(1)} %slice-done.1), channel_id=1, replica_groups=mesh['dp'=16,'rule'=32] {'dp'}, dimensions={0}, use_global_device_ids=true | all-gather | bytes 1044480 | tf_op jit(solution)/shard_map/all_gather | solution.py:304
  199.6 0.7 fusion.13
  200.3 2.2 %all-gather.5.cloned.1.call-done = bf16[2176,256]{1,0:T(8,128)(2,1)} async-done(((bf16[136,256]{1,0:T(8,128)(2,1)}), bf16[2176,256]{1,0:T(8,128)(2,1)}) %all-gather.5.cloned.1.call-update) | async-done | bytes 1114128 | tf_op jit(solution)/shard_map/all_gather | solution.py:305
  202.5 2.7 %fusion = bf16[256,512]{1,0:T(8,128)(2,1)} fusion(f32[256,512]{1,0:T(8,128)S(1)} %fusion.13, bf16[2176,256]{1,0:T(8,128)(2,1)} %all-gather.5.cloned.1.call-done, bf16[2176,512]{1,0:T(8,128)(2,1)S(1)} %bitcast.85), kind=kOutput, calls=%fused_computation.2 | convolution fusion | flops 570687488 | bytes 4128768 | tf_op jit(solution)/shard_map/dot_general | solution.py:18
  (37 shorter events, 4.1 us)
Async XLA Ops:
  7.2 23.0 %copy-start.2 = (bf16[8,8192]{1,0:T(8,128)(2,1)S(1)}, bf16[8,8192]{1,0:T(8,128)(2,1)}, u32[]{:S(2)}) copy-start(bf16[8,8192]{1,0:T(8,128)(2,1)} %attn_ref.1) | copy-start | bytes 393220
  7.2 23.0 %all-to-all-start = ((bf16[8,32,256]{2,0,1:T(8,128)(2,1)}), bf16[8,32,256]{2,0,1:T(8,128)(2,1)S(1)}, u32[]{:S(2)}, u32[]{:S(2)}) async-start(bf16[8,32,256]{2,0,1:T(8,128)(2,1)} %bitcast.87), calls=%async_computation | async-start | bytes 262144 | tf_op jit(solution)/shard_map/all_to_all | solution.py:271
  21.0 145.3 %all-gather.3.cloned.1.call-start = ((), (), s32[]{:S(2)}) async-start(), calls=%async_computation.6 | async-start | bytes 4325376 | tf_op jit(solution)/shard_map/all_gather | solution.py:286
  30.2 29.6 %copy-start.3 = (bf16[8,256,512]{2,1,0:T(8,128)(2,1)S(1)}, bf16[8,256,512]{2,1,0:T(8,128)(2,1)}, u32[]{:S(2)}) copy-start(bf16[8,256,512]{2,1,0:T(8,128)(2,1)} %weight_ref.3) | copy-start | bytes 6291460
  63.7 0.8 copy-start
  98.5 8.5 %copy-start.7 = (f32[8,512]{1,0:T(8,128)S(1)}, f32[8,512]{1,0:T(8,128)}, u32[]{:S(2)}) copy-start(f32[8,512]{1,0:T(8,128)} %param.14) | copy-start | bytes 49156
  98.5 8.5 %copy-start.8 = (f32[8,512]{1,0:T(8,128)S(1)}, f32[8,512]{1,0:T(8,128)}, u32[]{:S(2)}) copy-start(f32[8,512]{1,0:T(8,128)} %param.15) | copy-start | bytes 49156
  99.8 33.9 %all-to-all-start.3 = ((bf16[32,32,512]{2,1,0:T(8,128)(2,1)}), bf16[32,32,512]{2,1,0:T(8,128)(2,1)S(1)}, u32[]{:S(2)}, u32[]{:S(2)}) async-start(bf16[32,32,512]{2,1,0:T(8,128)(2,1)} %broadcast_in_dim.14), calls=%async_computation.3 | async-start | bytes 2097152 | tf_op jit(solution)/shard_map/all_to_all | solution.py:292
  106.9 95.6 %all-gather.5.cloned.1.call-start = ((), (), s32[]{:S(2)}) async-start(), calls=%async_computation.7 | async-start | bytes 1183744 | tf_op jit(solution)/shard_map/all_gather | solution.py:305
  133.7 1.6 copy-start.4
  139.8 31.3 %copy-start.1 = (bf16[1024,256]{1,0:T(8,128)(2,1)S(1)}, bf16[1024,256]{1,0:T(8,128)(2,1)}, u32[]{:S(2)}) copy-start(bf16[1024,256]{1,0:T(8,128)(2,1)} %copy-done) | copy-start | bytes 1572868
  166.4 12.3 %copy-start.6 = (bf16[256,256]{1,0:T(8,128)(2,1)}, bf16[256,256]{1,0:T(8,128)(2,1)S(1)}, u32[]{:S(2)}) copy-start(bf16[256,256]{1,0:T(8,128)(2,1)S(1)} %convolution_convert_fusion.1) | copy-start | bytes 393220
  167.8 9.9 %all-to-all-start.4 = ((bf16[16,1,64]{2,1,0:T(2,128)(2,1)}), bf16[16,1,64]{2,1,0:T(2,128)(2,1)S(1)}, u32[]{:S(2)}, u32[]{:S(2)}) async-start(bf16[16,1,64]{2,1,0:T(2,128)(2,1)} %all_to_all.56), calls=%async_computation.4 | async-start | bytes 16384 | tf_op jit(solution)/shard_map/all_to_all | solution.py:307
  177.8 2.2 %copy-start.5 = (bf16[16,256,512]{2,1,0:T(8,128)(2,1)S(1)}, bf16[16,256,512]{2,1,0:T(8,128)(2,1)}, u32[]{:S(2)}) copy-start(bf16[16,256,512]{2,1,0:T(8,128)(2,1)} %all-gather.3.cloned.1.call-done) | copy-start | bytes 12582916
  180.1 0.8 slice-start.1
  180.1 19.5 %slice-start = ((bf16[16,256,512]{2,1,0:T(8,128)(2,1)}), bf16[16,120,512]{2,1,0:T(8,128)(2,1)S(1)}, s32[]{:S(2)}) async-start(bf16[16,256,512]{2,1,0:T(8,128)(2,1)} %all-gather.3.cloned.1.call-done), calls=%async_computation.8 | async-start | bytes 3932160 | tf_op jit(solution)/shard_map/slice | solution.py:302
Sparse Core Ops, SparseCore 0:
  64.7 95.9 all-gather.2
  167.2 35.2 all-gather.4
